TPU v7x, 32 devices: a whole 2x2x4 slice. The times are simulated.
32 devices in a mesh: dp: 16 (over z, y, core), text: 2 (over x).
Axes of the slice: x: 2, y: 2, z: 4, core: 2. Of those that a mesh axis runs over, the one named last changes fastest.
Arguments:
- tokens_in: bfloat16 [8192, 2048], P(('dp', 'text')), may hold values from -6 to 6
- mask_flags: int32 [8192], P(('dp', 'text')), may hold values from 0 to 1, as said below
- text_states: bfloat16 [32, 128, 2048], P('dp', 'text'), may hold values from -6 to 6
- mask_embed: bfloat16 [2048], P(('dp', 'text')), may hold values from -6 to 6
- gain_attn: bfloat16 [2048], P(('dp', 'text')), may hold values from 0.25 to 1.75
- bias_attn: bfloat16 [2048], P(('dp', 'text')), may hold values from -3 to 3
- attn_query: bfloat16 [2048, 2048], P(('dp', 'text')), may hold values from -0.125 to 0.125
- attn_key: bfloat16 [2048, 2048], P(('dp', 'text')), may hold values from -0.125 to 0.125
- attn_value: bfloat16 [2048, 2048], P(('dp', 'text')), may hold values from -0.125 to 0.125
- attn_out: bfloat16 [2048, 2048], P(('dp', 'text')), may hold values from -2 to 2
- gain_cross: bfloat16 [2048], P(('dp', 'text')), may hold values from 0.25 to 1.75
- bias_cross: bfloat16 [2048], P(('dp', 'text')), may hold values from -3 to 3
- cross_query: bfloat16 [2048, 2048], P(('dp', 'text')), may hold values from -0.125 to 0.125
- cross_key: bfloat16 [2048, 2048], P(('dp', 'text')), may hold values from -0.125 to 0.125
- cross_value: bfloat16 [2048, 2048], P(('dp', 'text')), may hold values from -0.125 to 0.125
- cross_out: bfloat16 [2048, 2048], P(('dp', 'text')), may hold values from -1.5 to 1.5
- gain_mlp: bfloat16 [2048], P(('dp', 'text')), may hold values from 0.25 to 1.75
- bias_mlp: bfloat16 [2048], P(('dp', 'text')), may hold values from -3 to 3
- mlp_in: bfloat16 [2048, 8192], P(('dp', 'text')), may hold values from -0.125 to 0.125
- mlp_out: bfloat16 [8192, 2048], P(('dp', 'text')), may hold values from -0.0625 to 0.0625
- out_grad: bfloat16 [8192, 2048], P(('dp', 'text')), may hold values from -6 to 6
Outputs:
- output: bfloat16 [8192, 2048], P(('dp', 'text'))
- tokens_grad: float32 [8192, 2048], P(('dp', 'text'))
- text_grad: float32 [32, 128, 2048], P('dp', 'text')
- mask_embed_grad: float32 [2048], P(('dp', 'text'))
- gain_attn_grad: float32 [2048], P(('dp', 'text'))
- bias_attn_grad: float32 [2048], P(('dp', 'text'))
- attn_query_grad: float32 [2048, 2048], P(('dp', 'text'))
- attn_key_grad: float32 [2048, 2048], P(('dp', 'text'))
- attn_value_grad: float32 [2048, 2048], P(('dp', 'text'))
- attn_out_grad: float32 [2048, 2048], P(('dp', 'text'))
- gain_cross_grad: float32 [2048], P(('dp', 'text'))
- bias_cross_grad: float32 [2048], P(('dp', 'text'))
- cross_query_grad: float32 [2048, 2048], P(('dp', 'text'))
- cross_key_grad: float32 [2048, 2048], P(('dp', 'text'))
- cross_value_grad: float32 [2048, 2048], P(('dp', 'text'))
- cross_out_grad: float32 [2048, 2048], P(('dp', 'text'))
- gain_mlp_grad: float32 [2048], P(('dp', 'text'))
- bias_mlp_grad: float32 [2048], P(('dp', 'text'))
- mlp_in_grad: float32 [2048, 8192], P(('dp', 'text'))
- mlp_out_grad: float32 [8192, 2048], P(('dp', 'text'))
Inputs may be any that keep to these rules, and one draw needn't show every extreme that they name: `mask_flags`: for each image a masking ratio is drawn from a cosine plan, and a number of its 256 tokens between 1 and 256, set by that ratio, is flagged at positions drawn uniformly.
All inputs are finite; a program needn't handle non-finite values.
Results may differ from a plain program's by a relative error of at most 0.025.
Values may be sent and summed in bfloat16 or wider, within the bound.
No kernel may reach another device: no remote copies, remote signals or barrier semaphores. Data moves between devices by JAX's collectives and lax.ppermute only.
A program may use at most 576 MiB of HBM per device.

v0:
```python
import jax
import jax.numpy as jnp
from jax import lax
from jax.sharding import PartitionSpec as P

DH = 128
L = 256


epsilon = 1e-06


def normalize(rows):
    mean = jnp.mean(rows, axis=-1, keepdims=True)
    centered = rows - mean
    inverse = lax.rsqrt(jnp.mean(centered * centered, axis=-1, keepdims=True) + epsilon)
    return (centered * inverse, inverse)


def norm_backward(grad_out, unit_rows, inverse, gain):
    scaled = grad_out * gain
    mean_grad = jnp.mean(scaled, axis=-1, keepdims=True)
    mean_mixed = jnp.mean(scaled * unit_rows, axis=-1, keepdims=True)
    rows_grad = inverse * (scaled - mean_grad - unit_rows * mean_mixed)
    return (rows_grad, jnp.sum(grad_out * unit_rows, axis=0), jnp.sum(grad_out, axis=0))


def product(left, right):
    return jnp.dot(left, right, preferred_element_type=jnp.float32)


def outer_grad(left, right):
    return lax.dot_general(
        left, right, (((0,), (0,)), ((), ())), preferred_element_type=jnp.float32
    )


def back_project(left, right):
    return lax.dot_general(
        left, right, (((1,), (1,)), ((), ())), preferred_element_type=jnp.float32
    )


def attend_forward(queries, keys, values, head_scale):
    scores = (
        jnp.einsum("glhe,gche->ghlc", queries, keys, preferred_element_type=jnp.float32)
        * head_scale
    )
    top = jnp.max(scores, axis=-1, keepdims=True)
    exps = jnp.exp(scores - top)
    total = jnp.sum(exps, axis=-1, keepdims=True)
    weights = (exps / total).astype(jnp.bfloat16)
    mixed = jnp.einsum("ghlc,gche->glhe", weights, values, preferred_element_type=jnp.float32)
    return (mixed, (top + jnp.log(total))[..., 0])


def attend_backward(queries, keys, values, mixed_grad, log_total, delta, head_scale):
    scores = (
        jnp.einsum("glhe,gche->ghlc", queries, keys, preferred_element_type=jnp.float32)
        * head_scale
    )
    weights = jnp.exp(scores - log_total[..., None])
    values_grad = jnp.einsum(
        "ghlc,glhe->gche",
        weights.astype(jnp.bfloat16),
        mixed_grad,
        preferred_element_type=jnp.float32,
    )
    weight_grad = jnp.einsum(
        "glhe,gche->ghlc", mixed_grad, values, preferred_element_type=jnp.float32
    )
    delta = jnp.sum(weights * weight_grad, axis=-1)
    score_grad = (weights * (weight_grad - delta[..., None])).astype(jnp.bfloat16)
    queries_grad = (
        jnp.einsum("ghlc,gche->glhe", score_grad, keys, preferred_element_type=jnp.float32)
        * head_scale
    )
    keys_grad = (
        jnp.einsum("ghlc,glhe->gche", score_grad, queries, preferred_element_type=jnp.float32)
        * head_scale
    )
    return (queries_grad, keys_grad, values_grad)


def on_device(
    tokens_in,
    mask_flags,
    text_states,
    mask_embed,
    gain_attn,
    bias_attn,
    attn_query,
    attn_key,
    attn_value,
    attn_out,
    gain_cross,
    bias_cross,
    cross_query,
    cross_key,
    cross_value,
    cross_out,
    gain_mlp,
    bias_mlp,
    mlp_in,
    mlp_out,
    out_grad,
):
    width = attn_query.shape[1]
    head_size = DH
    heads = width // head_size
    rows = tokens_in.shape[0]
    images = rows // L
    head_scale = head_size ** (-0.5)
    group_images = text_states.shape[0]
    ctx_local = text_states.shape[1]
    (
        whole_embed,
        whole_gain_attn,
        whole_bias_attn,
        whole_query,
        whole_key,
        whole_value,
        whole_out,
        whole_gain_cross,
        whole_bias_cross,
        whole_cross_query,
        whole_cross_key,
        whole_cross_value,
        whole_cross_out,
    ) = (
        lax.all_gather(mask_embed, ("dp", "text"), axis=0, tiled=True),
        lax.all_gather(gain_attn, ("dp", "text"), axis=0, tiled=True),
        lax.all_gather(bias_attn, ("dp", "text"), axis=0, tiled=True),
        lax.all_gather(attn_query, ("dp", "text"), axis=0, tiled=True),
        lax.all_gather(attn_key, ("dp", "text"), axis=0, tiled=True),
        lax.all_gather(attn_value, ("dp", "text"), axis=0, tiled=True),
        lax.all_gather(attn_out, ("dp", "text"), axis=0, tiled=True),
        lax.all_gather(gain_cross, ("dp", "text"), axis=0, tiled=True),
        lax.all_gather(bias_cross, ("dp", "text"), axis=0, tiled=True),
        lax.all_gather(cross_query, ("dp", "text"), axis=0, tiled=True),
        lax.all_gather(cross_key, ("dp", "text"), axis=0, tiled=True),
        lax.all_gather(cross_value, ("dp", "text"), axis=0, tiled=True),
        lax.all_gather(cross_out, ("dp", "text"), axis=0, tiled=True),
    )
    masked = mask_flags[:, None] == 1
    start = jnp.where(
        masked, whole_embed.astype(jnp.float32)[None, :], tokens_in.astype(jnp.float32)
    )
    unit_one, inverse_one = normalize(start)
    normed_one = (
        unit_one * whole_gain_attn.astype(jnp.float32) + whole_bias_attn.astype(jnp.float32)
    ).astype(jnp.bfloat16)
    queries = (
        product(normed_one, whole_query).astype(jnp.bfloat16).reshape(images, L, heads, head_size)
    )
    keys = product(normed_one, whole_key).astype(jnp.bfloat16).reshape(images, L, heads, head_size)
    values = (
        product(normed_one, whole_value).astype(jnp.bfloat16).reshape(images, L, heads, head_size)
    )
    self_mixed, self_total = attend_forward(queries, keys, values, head_scale)
    self_flat = self_mixed.reshape(rows, width).astype(jnp.bfloat16)
    first = start + product(self_flat, whole_out)
    unit_two, inverse_two = normalize(first)
    normed_two = (
        unit_two * whole_gain_cross.astype(jnp.float32) + whole_bias_cross.astype(jnp.float32)
    ).astype(jnp.bfloat16)
    cross_queries = (
        product(normed_two, whole_cross_query)
        .astype(jnp.bfloat16)
        .reshape(images, L, heads, head_size)
    )
    text_rows = text_states.reshape(group_images * ctx_local, width)
    text_keys = (
        product(text_rows, whole_cross_key)
        .astype(jnp.bfloat16)
        .reshape(group_images, ctx_local, heads, head_size)
    )
    text_values = (
        product(text_rows, whole_cross_value)
        .astype(jnp.bfloat16)
        .reshape(group_images, ctx_local, heads, head_size)
    )
    own_keys, own_values = (
        lax.all_to_all(text_keys, "text", split_axis=0, concat_axis=1, tiled=True),
        lax.all_to_all(text_values, "text", split_axis=0, concat_axis=1, tiled=True),
    )
    own_mixed, cross_total = attend_forward(cross_queries, own_keys, own_values, head_scale)
    cross_flat = own_mixed.reshape(rows, width).astype(jnp.bfloat16)
    second = first + product(cross_flat, whole_cross_out)
    whole_gain_mlp, whole_bias_mlp, whole_mlp_in, whole_mlp_out = (
        lax.all_gather(gain_mlp, ("dp", "text"), axis=0, tiled=True),
        lax.all_gather(bias_mlp, ("dp", "text"), axis=0, tiled=True),
        lax.all_gather(mlp_in, ("dp", "text"), axis=0, tiled=True),
        lax.all_gather(mlp_out, ("dp", "text"), axis=0, tiled=True),
    )
    unit_three, inverse_three = normalize(second)
    normed_three = (
        unit_three * whole_gain_mlp.astype(jnp.float32) + whole_bias_mlp.astype(jnp.float32)
    ).astype(jnp.bfloat16)
    hidden_pre = product(normed_three, whole_mlp_in)
    activated = jax.nn.gelu(hidden_pre, approximate=False).astype(jnp.bfloat16)
    result = second + product(activated, whole_mlp_out)
    output = result.astype(jnp.bfloat16)
    back_gain_mlp, back_mlp_in, back_mlp_out = (
        lax.all_gather(gain_mlp, ("dp", "text"), axis=0, tiled=True),
        lax.all_gather(mlp_in, ("dp", "text"), axis=0, tiled=True),
        lax.all_gather(mlp_out, ("dp", "text"), axis=0, tiled=True),
    )
    activated_grad = back_project(out_grad, back_mlp_out)
    mlp_out_full = outer_grad(activated, out_grad)
    unused, gelu_pull = jax.vjp(lambda inner: jax.nn.gelu(inner, approximate=False), hidden_pre)
    hidden_grad = gelu_pull(activated_grad)[0].astype(jnp.bfloat16)
    normed_three_grad = back_project(hidden_grad, back_mlp_in)
    mlp_in_full = outer_grad(normed_three, hidden_grad)
    rows_three, gain_mlp_term, bias_mlp_term = norm_backward(
        normed_three_grad, unit_three, inverse_three, back_gain_mlp.astype(jnp.float32)
    )
    second_grad = out_grad.astype(jnp.float32) + rows_three
    gain_mlp_grad, bias_mlp_grad, mlp_in_grad, mlp_out_grad = (
        lax.psum_scatter(gain_mlp_term, ("dp", "text"), scatter_dimension=0, tiled=True),
        lax.psum_scatter(bias_mlp_term, ("dp", "text"), scatter_dimension=0, tiled=True),
        lax.psum_scatter(mlp_in_full, ("dp", "text"), scatter_dimension=0, tiled=True),
        lax.psum_scatter(mlp_out_full, ("dp", "text"), scatter_dimension=0, tiled=True),
    )
    (
        back_gain_attn,
        back_query,
        back_key,
        back_value,
        back_out,
        back_gain_cross,
        back_cross_query,
        back_cross_key,
        back_cross_value,
        back_cross_out,
    ) = (
        lax.all_gather(gain_attn, ("dp", "text"), axis=0, tiled=True),
        lax.all_gather(attn_query, ("dp", "text"), axis=0, tiled=True),
        lax.all_gather(attn_key, ("dp", "text"), axis=0, tiled=True),
        lax.all_gather(attn_value, ("dp", "text"), axis=0, tiled=True),
        lax.all_gather(attn_out, ("dp", "text"), axis=0, tiled=True),
        lax.all_gather(gain_cross, ("dp", "text"), axis=0, tiled=True),
        lax.all_gather(cross_query, ("dp", "text"), axis=0, tiled=True),
        lax.all_gather(cross_key, ("dp", "text"), axis=0, tiled=True),
        lax.all_gather(cross_value, ("dp", "text"), axis=0, tiled=True),
        lax.all_gather(cross_out, ("dp", "text"), axis=0, tiled=True),
    )
    second_low = second_grad.astype(jnp.bfloat16)
    cross_out_full = outer_grad(cross_flat, second_low)
    cross_mixed_grad = (
        back_project(second_low, back_cross_out)
        .astype(jnp.bfloat16)
        .reshape(images, L, heads, head_size)
    )
    cross_queries_grad, own_keys_grad, own_values_grad = attend_backward(
        cross_queries, own_keys, own_values, cross_mixed_grad, cross_total, None, head_scale
    )
    text_keys_low, text_values_low = (
        lax.all_to_all(
            own_keys_grad.astype(jnp.bfloat16), "text", split_axis=1, concat_axis=0, tiled=True
        ),
        lax.all_to_all(
            own_values_grad.astype(jnp.bfloat16), "text", split_axis=1, concat_axis=0, tiled=True
        ),
    )
    cross_queries_low = cross_queries_grad.reshape(rows, width).astype(jnp.bfloat16)
    normed_two_grad = back_project(cross_queries_low, back_cross_query)
    cross_query_full = outer_grad(normed_two, cross_queries_low)
    keys_rows_grad = text_keys_low.reshape(group_images * ctx_local, width)
    values_rows_grad = text_values_low.reshape(group_images * ctx_local, width)
    text_grad = back_project(keys_rows_grad, back_cross_key) + back_project(
        values_rows_grad, back_cross_value
    )
    cross_key_full = outer_grad(text_rows, keys_rows_grad)
    cross_value_full = outer_grad(text_rows, values_rows_grad)
    rows_two, gain_cross_term, bias_cross_term = norm_backward(
        normed_two_grad, unit_two, inverse_two, back_gain_cross.astype(jnp.float32)
    )
    first_grad = second_grad + rows_two
    first_low = first_grad.astype(jnp.bfloat16)
    attn_out_full = outer_grad(self_flat, first_low)
    self_mixed_grad = (
        back_project(first_low, back_out).astype(jnp.bfloat16).reshape(images, L, heads, head_size)
    )
    queries_grad, keys_grad, values_grad = attend_backward(
        queries, keys, values, self_mixed_grad, self_total, None, head_scale
    )
    queries_low = queries_grad.reshape(rows, width).astype(jnp.bfloat16)
    keys_low = keys_grad.reshape(rows, width).astype(jnp.bfloat16)
    values_low = values_grad.reshape(rows, width).astype(jnp.bfloat16)
    normed_one_grad = (
        back_project(queries_low, back_query)
        + back_project(keys_low, back_key)
        + back_project(values_low, back_value)
    )
    attn_query_full = outer_grad(normed_one, queries_low)
    attn_key_full = outer_grad(normed_one, keys_low)
    attn_value_full = outer_grad(normed_one, values_low)
    rows_one, gain_attn_term, bias_attn_term = norm_backward(
        normed_one_grad, unit_one, inverse_one, back_gain_attn.astype(jnp.float32)
    )
    start_grad = first_grad + rows_one
    tokens_grad = jnp.where(masked, 0.0, start_grad)
    embed_term = jnp.sum(jnp.where(masked, start_grad, 0.0), axis=0)
    (
        mask_embed_grad,
        gain_attn_grad,
        bias_attn_grad,
        attn_query_grad,
        attn_key_grad,
        attn_value_grad,
        attn_out_grad,
        gain_cross_grad,
        bias_cross_grad,
        cross_query_grad,
        cross_key_grad,
        cross_value_grad,
        cross_out_grad,
    ) = (
        lax.psum_scatter(embed_term, ("dp", "text"), scatter_dimension=0, tiled=True),
        lax.psum_scatter(gain_attn_term, ("dp", "text"), scatter_dimension=0, tiled=True),
        lax.psum_scatter(bias_attn_term, ("dp", "text"), scatter_dimension=0, tiled=True),
        lax.psum_scatter(attn_query_full, ("dp", "text"), scatter_dimension=0, tiled=True),
        lax.psum_scatter(attn_key_full, ("dp", "text"), scatter_dimension=0, tiled=True),
        lax.psum_scatter(attn_value_full, ("dp", "text"), scatter_dimension=0, tiled=True),
        lax.psum_scatter(attn_out_full, ("dp", "text"), scatter_dimension=0, tiled=True),
        lax.psum_scatter(gain_cross_term, ("dp", "text"), scatter_dimension=0, tiled=True),
        lax.psum_scatter(bias_cross_term, ("dp", "text"), scatter_dimension=0, tiled=True),
        lax.psum_scatter(cross_query_full, ("dp", "text"), scatter_dimension=0, tiled=True),
        lax.psum_scatter(cross_key_full, ("dp", "text"), scatter_dimension=0, tiled=True),
        lax.psum_scatter(cross_value_full, ("dp", "text"), scatter_dimension=0, tiled=True),
        lax.psum_scatter(cross_out_full, ("dp", "text"), scatter_dimension=0, tiled=True),
    )
    return (
        output,
        tokens_grad,
        text_grad.reshape(text_states.shape),
        mask_embed_grad,
        gain_attn_grad,
        bias_attn_grad,
        attn_query_grad,
        attn_key_grad,
        attn_value_grad,
        attn_out_grad,
        gain_cross_grad,
        bias_cross_grad,
        cross_query_grad,
        cross_key_grad,
        cross_value_grad,
        cross_out_grad,
        gain_mlp_grad,
        bias_mlp_grad,
        mlp_in_grad,
        mlp_out_grad,
    )


def solution(mesh):
    return jax.shard_map(
        on_device,
        mesh=mesh,
        in_specs=(
            P(("dp", "text"), None),
            P(("dp", "text")),
            P("dp", "text", None),
            P(("dp", "text")),
            P(("dp", "text")),
            P(("dp", "text")),
            P(("dp", "text"), None),
            P(("dp", "text"), None),
            P(("dp", "text"), None),
            P(("dp", "text"), None),
            P(("dp", "text")),
            P(("dp", "text")),
            P(("dp", "text"), None),
            P(("dp", "text"), None),
            P(("dp", "text"), None),
            P(("dp", "text"), None),
            P(("dp", "text")),
            P(("dp", "text")),
            P(("dp", "text"), None),
            P(("dp", "text"), None),
            P(("dp", "text"), None),
        ),
        out_specs=(
            P(("dp", "text"), None),
            P(("dp", "text"), None),
            P("dp", "text", None),
            P(("dp", "text")),
            P(("dp", "text")),
            P(("dp", "text")),
            P(("dp", "text"), None),
            P(("dp", "text"), None),
            P(("dp", "text"), None),
            P(("dp", "text"), None),
            P(("dp", "text")),
            P(("dp", "text")),
            P(("dp", "text"), None),
            P(("dp", "text"), None),
            P(("dp", "text"), None),
            P(("dp", "text"), None),
            P(("dp", "text")),
            P(("dp", "text")),
            P(("dp", "text"), None),
            P(("dp", "text"), None),
        ),
        check_vma=False,
    )
```

profile of v0, /device:TPU:3, one launch (start us, length us, event | category | flops | bytes accessed | tf_op | source)
XLA Modules:
  0.0 6841.3 jit_solution(10749770524843686828)
XLA Ops:
  15.9 40.4 all-reduce.15
  57.4 32.9 all-gather.23.cloned.1.call-done
  99.6 71.2 %all-gather.15.cloned.1.call-done = bf16[2048,2048]{1,0:T(8,128)(2,1)} async-done(((bf16[64,2048]{1,0:T(8,128)(2,1)}), bf16[2048,2048]{1,0:T(8,128)(2,1)}) %all-gather.15.cloned.1.call-update) | async-done | bytes 8388624 | tf_op jit(solution)/shard_map/all_gather | solution.py:135
  179.2 70.6 %all-gather.13.cloned.1.call-done = bf16[2048,2048]{1,0:T(8,128)(2,1)} async-done(((bf16[64,2048]{1,0:T(8,128)(2,1)}), bf16[2048,2048]{1,0:T(8,128)(2,1)}) %all-gather.13.cloned.1.call-update) | async-done | bytes 8388624 | tf_op jit(solution)/shard_map/all_gather | solution.py:134
  263.8 64.7 all-gather.11.cloned.1.call-done
  336.7 70.7 %all-gather.17.cloned.1.call-done = bf16[2048,2048]{1,0:T(8,128)(2,1)} async-done(((bf16[64,2048]{1,0:T(8,128)(2,1)}), bf16[2048,2048]{1,0:T(8,128)(2,1)}) %all-gather.17.cloned.1.call-update) | async-done | bytes 8388624 | tf_op jit(solution)/shard_map/all_gather | solution.py:137
  414.9 71.2 %all-gather.21.cloned.1.call-done = bf16[2048,2048]{1,0:T(8,128)(2,1)} async-done(((bf16[64,2048]{1,0:T(8,128)(2,1)}), bf16[2048,2048]{1,0:T(8,128)(2,1)}) %all-gather.21.cloned.1.call-update) | async-done | bytes 8388624 | tf_op jit(solution)/shard_map/all_gather | solution.py:140
  492.6 72.4 %all-gather.19.cloned.1.call-done = bf16[2048,2048]{1,0:T(8,128)(2,1)} async-done(((bf16[64,2048]{1,0:T(8,128)(2,1)}), bf16[2048,2048]{1,0:T(8,128)(2,1)}) %all-gather.19.cloned.1.call-update) | async-done | bytes 8388624 | tf_op jit(solution)/shard_map/all_gather | solution.py:142
  588.1 57.4 all-gather.25.cloned.1.call-done
  653.4 188.6 %all-gather.27.cloned.1.call-done = bf16[2048,8192]{1,0:T(8,128)(2,1)} async-done(((bf16[64,8192]{1,0:T(8,128)(2,1)}), bf16[2048,8192]{1,0:T(8,128)(2,1)}) %all-gather.27.cloned.1.call-update) | async-done | bytes 33554448 | tf_op jit(solution)/shard_map/all_gather | solution.py:193
  860.5 177.3 %all-gather.29.cloned.1.call-done = bf16[8192,2048]{1,0:T(8,128)(2,1)} async-done(((bf16[256,2048]{1,0:T(8,128)(2,1)}), bf16[8192,2048]{1,0:T(8,128)(2,1)}) %all-gather.29.cloned.1.call-update) | async-done | bytes 33554448 | tf_op jit(solution)/shard_map/all_gather | solution.py:194
  1037.8 33.6 add_convert_fusion
  1291.2 27.2 fusion.61
  1372.7 43.2 all-reduce.14
  1454.2 33.0 reduce-scatter.23.cloned.1.call-done
  1487.1 361.3 %reduce-scatter.21.cloned.1.call-done = f32[64,2048]{1,0:T(8,128)} async-done(((f32[2048,2048]{1,0:T(8,128)}), f32[64,2048]{1,0:T(8,128)}) %reduce-scatter.21.cloned.1.call-update) | async-done | bytes 524304 | tf_op jit(solution)/shard_map/reduce_scatter | solution.py:326
  1848.5 361.5 %reduce-scatter.25.cloned.1.call-done = f32[64,2048]{1,0:T(8,128)} async-done(((f32[2048,2048]{1,0:T(8,128)}), f32[64,2048]{1,0:T(8,128)}) %reduce-scatter.25.cloned.1.call-update) | async-done | bytes 524304 | tf_op jit(solution)/shard_map/reduce_scatter | solution.py:332
  2210.0 361.4 %reduce-scatter.19.cloned.1.call-done = f32[64,2048]{1,0:T(8,128)} async-done(((f32[2048,2048]{1,0:T(8,128)}), f32[64,2048]{1,0:T(8,128)}) %reduce-scatter.19.cloned.1.call-update) | async-done | bytes 524304 | tf_op jit(solution)/shard_map/reduce_scatter | solution.py:325
  2571.4 361.4 %reduce-scatter.17.cloned.1.call-done = f32[64,2048]{1,0:T(8,128)} async-done(((f32[2048,2048]{1,0:T(8,128)}), f32[64,2048]{1,0:T(8,128)}) %reduce-scatter.17.cloned.1.call-update) | async-done | bytes 524304 | tf_op jit(solution)/shard_map/reduce_scatter | solution.py:324
  2932.7 361.4 %reduce-scatter.15.cloned.1.call-done = f32[64,2048]{1,0:T(8,128)} async-done(((f32[2048,2048]{1,0:T(8,128)}), f32[64,2048]{1,0:T(8,128)}) %reduce-scatter.15.cloned.1.call-update) | async-done | bytes 524304 | tf_op jit(solution)/shard_map/reduce_scatter | solution.py:323
  3294.1 361.4 %reduce-scatter.33.cloned.1.call-done = f32[64,2048]{1,0:T(8,128)} async-done(((f32[2048,2048]{1,0:T(8,128)}), f32[64,2048]{1,0:T(8,128)}) %reduce-scatter.33.cloned.1.call-update) | async-done | bytes 524304
  3655.5 361.4 %reduce-scatter.31.cloned.1.call-done = f32[64,2048]{1,0:T(8,128)} async-done(((f32[2048,2048]{1,0:T(8,128)}), f32[64,2048]{1,0:T(8,128)}) %reduce-scatter.31.cloned.1.call-update) | async-done | bytes 524304
  4016.9 1409.0 %reduce-scatter.27.cloned.1.call-done = f32[64,8192]{1,0:T(8,128)} async-done(((f32[2048,8192]{1,0:T(8,128)}), f32[64,8192]{1,0:T(8,128)}) %reduce-scatter.27.cloned.1.call-update) | async-done | bytes 2097168 | tf_op jit(solution)/shard_map/reduce_scatter | solution.py:222
  5425.9 1408.2 %reduce-scatter.29.cloned.1.call-done = f32[256,2048]{1,0:T(8,128)} async-done(((f32[8192,2048]{1,0:T(8,128)}), f32[256,2048]{1,0:T(8,128)}) %reduce-scatter.29.cloned.1.call-update) | async-done | bytes 2097168 | tf_op jit(solution)/shard_map/reduce_scatter | solution.py:223
  (314 shorter events, 424.1 us)
Async XLA Ops:
  7.3 83.0 %all-gather.23.cloned.1.call-start = ((), (), s32[]{:S(2)}) async-start(), calls=%async_computation.20 | async-start | bytes 8650752 | tf_op jit(solution)/shard_map/all_gather | solution.py:141
  8.0 162.8 %all-gather.15.cloned.1.call-start = ((), (), s32[]{:S(2)}) async-start(), calls=%async_computation.16 | async-start | bytes 8650752 | tf_op jit(solution)/shard_map/all_gather | solution.py:135
  8.8 241.0 %all-gather.13.cloned.1.call-start = ((), (), s32[]{:S(2)}) async-start(), calls=%async_computation.15 | async-start | bytes 8650752 | tf_op jit(solution)/shard_map/all_gather | solution.py:134
  9.5 319.0 %all-gather.11.cloned.1.call-start = ((), (), s32[]{:S(2)}) async-start(), calls=%async_computation.14 | async-start | bytes 8650752 | tf_op jit(solution)/shard_map/all_gather | solution.py:136
  10.1 397.3 %all-gather.17.cloned.1.call-start = ((), (), s32[]{:S(2)}) async-start(), calls=%async_computation.17 | async-start | bytes 8650752 | tf_op jit(solution)/shard_map/all_gather | solution.py:137
  10.7 475.4 %all-gather.21.cloned.1.call-start = ((), (), s32[]{:S(2)}) async-start(), calls=%async_computation.19 | async-start | bytes 8650752 | tf_op jit(solution)/shard_map/all_gather | solution.py:140
  11.3 553.7 %all-gather.19.cloned.1.call-start = ((), (), s32[]{:S(2)}) async-start(), calls=%async_computation.18 | async-start | bytes 8650752 | tf_op jit(solution)/shard_map/all_gather | solution.py:142
  12.0 633.6 %all-gather.25.cloned.1.call-start = ((), (), s32[]{:S(2)}) async-start(), calls=%async_computation.21 | async-start | bytes 8650752 | tf_op jit(solution)/shard_map/all_gather | solution.py:143
  12.8 829.2 %all-gather.27.cloned.1.call-start = ((), (), s32[]{:S(2)}) async-start(), calls=%async_computation.22 | async-start | bytes 34603008 | tf_op jit(solution)/shard_map/all_gather | solution.py:193
  13.5 1024.3 %all-gather.29.cloned.1.call-start = ((), (), s32[]{:S(2)}) async-start(), calls=%async_computation.23 | async-start | bytes 34603008 | tf_op jit(solution)/shard_map/all_gather | solution.py:194
  56.4 429.7 %copy-start.50 = (f32[2048]{0:T(1024)}, f32[2048]{0:T(1024)S(1)}, u32[]{:S(2)}) copy-start(f32[2048]{0:T(1024)S(1)} %convert_element_type.206) | copy-start | bytes 24580
  56.4 785.6 %copy-start.44 = (f32[2048]{0:T(1024)}, f32[2048]{0:T(1024)S(1)}, u32[]{:S(2)}) copy-start(f32[2048]{0:T(1024)S(1)} %convert_element_type.217) | copy-start | bytes 24580
  95.8 475.3 %all-to-all-start.1 = ((bf16[2,64,16,128]{3,2,1,0:T(8,128)(2,1)}), bf16[2,64,16,128]{3,2,1,0:T(8,128)(2,1)S(1)}, u32[]{:S(2)}, u32[]{:S(2)}) async-start(bf16[2,64,16,128]{3,2,1,0:T(8,128)(2,1)} %bitcast.57), calls=%async_computation.1 | async-start | bytes 1048576 | tf_op jit(solution)/shard_map/all_to_all | solution.py:184
  571.1 12.7 all-to-all-start
  574.9 912.2 %reduce-scatter.23.cloned.1.call-start = ((), (), s32[]{:S(2)}) async-start(), calls=%async_computation.28 | async-start | bytes 17301504 | tf_op jit(solution)/shard_map/reduce_scatter | solution.py:329
  1118.1 730.4 %reduce-scatter.21.cloned.1.call-start = ((), (), s32[]{:S(2)}) async-start(), calls=%async_computation.27 | async-start | bytes 17301504 | tf_op jit(solution)/shard_map/reduce_scatter | solution.py:326
  1135.9 1074.1 %reduce-scatter.25.cloned.1.call-start = ((), (), s32[]{:S(2)}) async-start(), calls=%async_computation.29 | async-start | bytes 17301504 | tf_op jit(solution)/shard_map/reduce_scatter | solution.py:332
  1146.9 1424.4 %reduce-scatter.19.cloned.1.call-start = ((), (), s32[]{:S(2)}) async-start(), calls=%async_computation.26 | async-start | bytes 17301504 | tf_op jit(solution)/shard_map/reduce_scatter | solution.py:325
  1169.6 1763.1 %reduce-scatter.17.cloned.1.call-start = ((), (), s32[]{:S(2)}) async-start(), calls=%async_computation.25 | async-start | bytes 17301504 | tf_op jit(solution)/shard_map/reduce_scatter | solution.py:324
  1185.3 2108.8 %reduce-scatter.15.cloned.1.call-start = ((), (), s32[]{:S(2)}) async-start(), calls=%async_computation.24 | async-start | bytes 17301504 | tf_op jit(solution)/shard_map/reduce_scatter | solution.py:323
  1197.9 2457.6 %reduce-scatter.33.cloned.1.call-start = ((), (), s32[]{:S(2)}) async-start(), calls=%async_computation.33 | async-start | bytes 17301504
  1244.8 2772.1 %reduce-scatter.31.cloned.1.call-start = ((), (), s32[]{:S(2)}) async-start(), calls=%async_computation.32 | async-start | bytes 17301504
  1290.5 4135.3 %reduce-scatter.27.cloned.1.call-start = ((), (), s32[]{:S(2)}) async-start(), calls=%async_computation.30 | async-start | bytes 69206016 | tf_op jit(solution)/shard_map/reduce_scatter | solution.py:222
  1318.4 5515.6 %reduce-scatter.29.cloned.1.call-start = ((), (), s32[]{:S(2)}) async-start(), calls=%async_computation.31 | async-start | bytes 69206016 | tf_op jit(solution)/shard_map/reduce_scatter | solution.py:223
  (78 other events, 3129.1 us)
Sparse Core Ops, SparseCore 0:
  11.1 79.1 all-gather.22
  93.3 77.5 all-gather.14
  173.9 75.8 all-gather.12
  252.6 75.8 all-gather.10
  331.3 75.9 all-gather.16
  410.2 75.8 all-gather.20
  489.1 75.8 all-gather.18
  568.0 77.5 all-gather.24
  648.6 193.3 all-gather.26
  844.8 192.9 all-gather.28
  1118.2 368.8 reduce-scatter.22
  1489.9 358.5 reduce-scatter.20
  1851.3 358.6 reduce-scatter.24
  2212.7 358.6 reduce-scatter.18
  2574.1 358.6 reduce-scatter.16
  2935.5 358.6 reduce-scatter.14
  3296.8 358.6 reduce-scatter.32
  3658.2 358.6 reduce-scatter.30
  4019.8 1406.0 reduce-scatter.26
  5428.6 1405.3 reduce-scatter.28
where the time goes:
time: 6850 us; the launch traced here: 6840 us
  waiting for transfers between devices  6270 us (92%)
  matrix products  329 us (5%)
  blocking collectives  117 us (2%)
  local copies, waits for them, and re-layouts  76.8 us (1%)
    reduce_scatter x1, waiting for transfers between devices, on_device(): lax.psum_scatter(mlp_in_full, ('dp', 'text'), scatter_dimension=0, tiled=...  1410 us
    reduce_scatter x1, waiting for transfers between devices, on_device(): lax.psum_scatter(mlp_out_full, ('dp', 'text'), scatter_dimension=0, tiled...  1410 us
    unnamed x22, waiting for transfers between devices  729 us
    reduce_scatter x1, waiting for transfers between devices, on_device(): lax.psum_scatter(cross_out_full, ('dp', 'text'), scatter_dimension=0, til...  362 us
    reduce_scatter x1, waiting for transfers between devices, on_device(): lax.psum_scatter(attn_value_full, ('dp', 'text'), scatter_dimension=0, ti...  361 us
    reduce_scatter x1, waiting for transfers between devices, on_device(): lax.psum_scatter(attn_query_full, ('dp', 'text'), scatter_dimension=0, ti...  361 us
    reduce_scatter x1, waiting for transfers between devices, on_device(): lax.psum_scatter(attn_key_full, ('dp', 'text'), scatter_dimension=0, tile...  361 us
    reduce_scatter x1, waiting for transfers between devices, on_device(): lax.psum_scatter(attn_out_full, ('dp', 'text'), scatter_dimension=0, tile...  361 us
  transfers between devices with their start and end apart: 22, of which 21 were waited for; matrix products, arithmetic and copies ran while one was open for 5% of the time, Pallas kernels for 0%

commit v1 on v0

v1 whole, which is shorter than its diff:
```python
import functools

import jax
import jax.numpy as jnp
from jax import lax
from jax.experimental import pallas as pl
from jax.experimental.pallas import tpu as pltpu
from jax.sharding import PartitionSpec as P

DH = 128
L = 256
AXES = ("g", "core", "x")
F32 = jnp.float32
BF16 = jnp.bfloat16
epsilon = 1e-06


def normalize(rows):
    mean = jnp.mean(rows, axis=-1, keepdims=True)
    centered = rows - mean
    inverse = lax.rsqrt(jnp.mean(centered * centered, axis=-1, keepdims=True) + epsilon)
    return (centered * inverse, inverse)


def norm_backward(grad_out, unit_rows, inverse, gain):
    scaled = grad_out * gain
    mean_grad = jnp.mean(scaled, axis=-1, keepdims=True)
    mean_mixed = jnp.mean(scaled * unit_rows, axis=-1, keepdims=True)
    rows_grad = inverse * (scaled - mean_grad - unit_rows * mean_mixed)
    return (rows_grad, jnp.sum(grad_out * unit_rows, axis=0), jnp.sum(grad_out, axis=0))


def product(left, right):
    return jnp.dot(left, right, preferred_element_type=F32)


def outer_grad(left, right):
    return lax.dot_general(left, right, (((0,), (0,)), ((), ())), preferred_element_type=F32)


def back_project(left, right):
    return lax.dot_general(left, right, (((1,), (1,)), ((), ())), preferred_element_type=F32)


def forward_head(query, key, value, scale):
    scores = back_project(query, key) * scale
    exps = jnp.exp(scores - jnp.max(scores, axis=1, keepdims=True))
    weights = exps * (1.0 / jnp.sum(exps, axis=1, keepdims=True))
    return product(weights.astype(BF16), value).astype(BF16)


def backward_head(query, key, value, mixed_grad, scale):
    scores = back_project(key, query) * scale
    exps = jnp.exp(scores - jnp.max(scores, axis=0, keepdims=True))
    weights = exps * (1.0 / jnp.sum(exps, axis=0, keepdims=True))
    value_grad = product(weights.astype(BF16), mixed_grad)
    weight_grad = back_project(value, mixed_grad)
    delta = jnp.sum(weights * weight_grad, axis=0, keepdims=True)
    score_grad = (weights * (weight_grad - delta)).astype(BF16)
    query_grad = outer_grad(score_grad, key) * scale
    key_grad = product(score_grad, query) * scale
    return (query_grad.astype(BF16), key_grad.astype(BF16), value_grad.astype(BF16))


def self_forward_kernel(width, scale, qkv, mixed):
    for low in range(0, width, DH):
        at = [slice(part * width + low, part * width + low + DH) for part in range(3)]
        mixed[:, at[0]] = forward_head(qkv[:, at[0]], qkv[:, at[1]], qkv[:, at[2]], scale)


def self_backward_kernel(width, scale, qkv, mixed_grad, grads):
    for low in range(0, width, DH):
        at = [slice(part * width + low, part * width + low + DH) for part in range(3)]
        terms = backward_head(
            qkv[:, at[0]], qkv[:, at[1]], qkv[:, at[2]], mixed_grad[:, at[0]], scale
        )
        for part in range(3):
            grads[:, at[part]] = terms[part]


def cross_forward_kernel(width, scale, queries, text, mixed):
    for low in range(0, width, DH):
        at = [slice(part * width + low, part * width + low + DH) for part in range(2)]
        mixed[:, at[0]] = forward_head(queries[:, at[0]], text[:, at[0]], text[:, at[1]], scale)


def cross_backward_kernel(width, scale, queries, text, mixed_grad, query_grads, text_grads):
    for low in range(0, width, DH):
        at = [slice(part * width + low, part * width + low + DH) for part in range(2)]
        terms = backward_head(
            queries[:, at[0]], text[:, at[0]], text[:, at[1]], mixed_grad[:, at[0]], scale
        )
        query_grads[:, at[0]] = terms[0]
        text_grads[:, at[0]] = terms[1]
        text_grads[:, at[1]] = terms[2]


def by_image(kernel, args, blocks, shapes, out_blocks, flops, skip=0):
    images = shapes[0][0] // out_blocks[0][0]
    offsets = [0 if arg.shape[0] // block[0] == images else skip for arg, block in zip(args, blocks)]
    total = sum(images * block[0] * block[1] * 2 for block in (*blocks, *out_blocks))
    return pl.pallas_call(
        kernel,
        grid=(images,),
        in_specs=[
            pl.BlockSpec(block, functools.partial(lambda off, i: (i + off, 0), off))
            for block, off in zip(blocks, offsets)
        ],
        out_specs=[pl.BlockSpec(block, lambda i: (i, 0)) for block in out_blocks],
        out_shape=[jax.ShapeDtypeStruct(shape, BF16) for shape in shapes],
        compiler_params=pltpu.CompilerParams(vmem_limit_bytes=32 * 1024 * 1024),
        cost_estimate=pl.CostEstimate(
            flops=flops, bytes_accessed=total, transcendentals=flops // 512
        ),
    )(*args)


def head_start(piece, rank):
    return DH * (4 * piece + 2 * (rank & 1) + (rank >> 1))


def hidden_start(size, piece, rank):
    return size * (4 * piece + rank)


def lanes_at(start, size):
    return pl.ds(pl.multiple_of(start, 128), size)


def cut_kernel(start, pieces, size, rank_ref, *refs):
    weights, (own, to_x, to_core) = refs[:-3], refs[-3:]
    for rel, out in ((0, own), (1, to_x.at[0]), (3, to_x.at[1]), (2, to_core)):
        rank = rank_ref[0] ^ rel
        for k, weight in enumerate(weights):
            for piece in range(pieces):
                column = (k * pieces + piece) * size
                out[:, column : column + size] = weight[:, lanes_at(start(piece, rank), size)]


def join_kernel(start, pieces, size, rank_ref, own, from_x, from_core, *outs):
    for rel, source in ((0, own), (1, from_x.at[0]), (2, from_core.at[0]), (3, from_core.at[1])):
        rank = rank_ref[0] ^ rel
        for k, out in enumerate(outs):
            for piece in range(pieces):
                column = (k * pieces + piece) * size
                value = source[:, column : column + size].astype(F32)
                out[:, lanes_at(start(piece, rank), size)] = value


def order_kernel(rank_ref, own, from_x, from_core, *refs):
    extra, (first, second) = refs[:-2], refs[-2:]
    rows, columns = own.shape
    lane = first.shape[1]
    for rel, source in ((0, own), (1, from_x.at[0]), (2, from_core.at[0]), (3, from_core.at[1])):
        at = pl.ds(pl.multiple_of((rank_ref[0] ^ rel) * rows, rows), rows)
        first[at, :] = source[:, :lane]
        second[at, : columns - lane] = source[:, lane:]
    for weight in extra:
        size = weight.shape[1] // 4
        for part in range(4):
            piece = weight[:, part * size : (part + 1) * size]
            second[part * rows : (part + 1) * rows, columns - lane :] = piece


def assemble_kernel(plan, count, places_ref, *refs):
    sources, outs, sems = refs[:count], refs[count:-1], refs[-1]
    copies = []
    for piece, place, moves in plan:
        for rows, columns, out, to_rows, to_columns in moves:
            copies.append(
                pltpu.make_async_copy(
                    sources[piece].at[pl.ds(*rows), pl.ds(*columns)],
                    outs[out].at[places_ref[place], pl.ds(*to_rows), pl.ds(*to_columns)],
                    sems.at[len(copies)],
                )
            )
            copies[-1].start()
    for copy in copies:
        copy.wait()


def whole_call(kernel, rank, args, shapes, dtype):
    moved = 2 * sum(arg.size * arg.dtype.itemsize for arg in args)
    return pl.pallas_call(
        kernel,
        in_specs=[pl.BlockSpec(memory_space=pltpu.SMEM)]
        + [pl.BlockSpec(memory_space=pltpu.VMEM)] * len(args),
        out_specs=[pl.BlockSpec(memory_space=pltpu.VMEM)] * len(shapes),
        out_shape=[jax.ShapeDtypeStruct(shape, dtype) for shape in shapes],
        compiler_params=pltpu.CompilerParams(vmem_limit_bytes=24 * 1024 * 1024),
        cost_estimate=pl.CostEstimate(flops=0, bytes_accessed=moved, transcendentals=0),
    )(rank, *args)


def assemble(plan, places, pieces, shapes):
    count = sum(len(moves) for piece, place, moves in plan)
    moved = 2 * sum(piece.size * piece.dtype.itemsize for piece in pieces)
    return pl.pallas_call(
        functools.partial(assemble_kernel, plan, len(pieces)),
        in_specs=[pl.BlockSpec(memory_space=pltpu.SMEM)]
        + [pl.BlockSpec(memory_space=pltpu.VMEM)] * len(pieces),
        out_specs=[pl.BlockSpec(memory_space=pl.ANY)] * len(shapes),
        out_shape=[jax.ShapeDtypeStruct(shape, BF16) for shape in shapes],
        scratch_shapes=[pltpu.SemaphoreType.DMA((count,))],
        compiler_params=pltpu.CompilerParams(vmem_limit_bytes=24 * 1024 * 1024),
        cost_estimate=pl.CostEstimate(flops=0, bytes_accessed=moved, transcendentals=0),
    )(places, *pieces)


def on_device(
    n_g,
    tokens_in,
    mask_flags,
    text_states,
    mask_embed,
    gain_attn,
    bias_attn,
    attn_query,
    attn_key,
    attn_value,
    attn_out,
    gain_cross,
    bias_cross,
    cross_query,
    cross_key,
    cross_value,
    cross_out,
    gain_mlp,
    bias_mlp,
    mlp_in,
    mlp_out,
    out_grad,
):
    n = n_g * 4
    half_ring = n_g // 2
    rows, width = tokens_in.shape
    own_rows = attn_query.shape[0]
    hidden = mlp_in.shape[1]
    heads = width // DH
    rank_heads = heads // 4
    rank_width = rank_heads * DH
    parts = n // heads
    ctx = 2 * text_states.shape[1]
    images = rows // L
    scale = DH ** (-0.5)

    g = lax.axis_index("g")
    core = lax.axis_index("core")
    x = lax.axis_index("x")

    order = list(range(0, n_g, 2)) + list(range(n_g - 1, 0, -2))
    ahead = {order[p]: order[(p + 1) % n_g] for p in range(n_g)}
    swap_x = [(i, i ^ 1) for i in range(n)]
    swap_core = [(i, i ^ 2) for i in range(n)]
    go_next = [(i, ahead[i // 4] * 4 + i % 4) for i in range(n)]
    go_prev = [(j, i) for i, j in go_next]
    place = jnp.where((g & 1) == 0, g >> 1, n_g - 1 - (g >> 1))

    def g_at(offset):
        p = place + (offset % n_g)
        p = jnp.where(p >= n_g, p - n_g, p)
        return jnp.where(p < half_ring, 2 * p, 2 * (n_g - 1 - p) + 1)

    def send(value, pairs):
        return lax.ppermute(value, AXES, pairs)

    token = mask_flags

    def pin(*values):
        nonlocal token
        values, token = lax.optimization_barrier((values, token))
        return values if len(values) > 1 else values[0]

    def flip(blocks):
        blocks = [jnp.where(x == 1, blocks[k ^ 1], blocks[k]) for k in range(4)]
        return [jnp.where(core == 1, blocks[k ^ 2], blocks[k]) for k in range(4)]

    me = g * 4 + core * 2 + x
    rank = jnp.reshape(core * 2 + x, (1,)).astype(jnp.int32)
    lane = width // 2
    hidden_rows = mlp_out.shape[0]
    head_cut = (head_start, rank_heads, DH)
    hidden_cut = (functools.partial(hidden_start, hidden_rows), n_g, hidden_rows)

    def pieces_of(cut, size):
        return [[int(cut[0](piece, to)) for piece in range(cut[1])] for to in range(4)]

    def cut_columns(weights, cut):
        start, pieces, size = cut
        if size % 128 == 0:
            shape = (own_rows, len(weights) * pieces * size)
            kernel = functools.partial(cut_kernel, start, pieces, size)
            return whole_call(kernel, pin(rank), weights, [shape, (2,) + shape, shape], BF16)
        rel = flip(
            [
                jnp.concatenate(
                    [weight[:, low : low + size] for weight in weights for low in lows], axis=1
                )
                for lows in pieces_of(cut, size)
            ]
        )
        return (rel[0], jnp.stack([rel[1], rel[3]]), rel[2])

    def join_columns(own, from_x, from_core, cut, count):
        start, pieces, size = cut
        if size % 128 == 0:
            shape = (own_rows, 4 * pieces * size)
            kernel = functools.partial(join_kernel, start, pieces, size)
            return whole_call(kernel, rank, [own, from_x, from_core], [shape] * count, F32)
        blocks = flip([own, from_x[0], from_core[0], from_core[1]])
        outs = []
        for k in range(count):
            found = sorted(
                (low, to, k * pieces + piece)
                for to, lows in enumerate(pieces_of(cut, size))
                for piece, low in enumerate(lows)
            )
            parts = [blocks[to][:, at * size : (at + 1) * size] for low, to, at in found]
            outs.append(jnp.concatenate(parts, axis=1).astype(F32))
        return outs

    def exchange_x(blocks):
        own, to_x, to_core = blocks
        return (own, to_core, send(to_x, swap_x))

    def exchange_core(state):
        own, to_core, from_x = state
        from_x = pin(from_x)
        return (own, from_x, send(jnp.stack([to_core, from_x[1]]), swap_core))

    def exchange_end(state):
        own, from_x, from_core = state
        return (own, from_x, pin(from_core))

    def in_order(state, *extra):
        shapes = [(4 * own_rows, lane)] * 2
        return whole_call(order_kernel, rank, list(exchange_end(state)) + list(extra), shapes, BF16)

    pieces = {}
    lanes_left = {"self": 2, "cross": 2, "in": 2, "down": 2}
    sums = {}
    places = jnp.stack([g_at(offset) for offset in range(n_g)]).astype(jnp.int32)

    def gather_task(name, side, block):
        found = pieces.setdefault((name, side), [])
        found.append((block, 0, 0))
        clock = counter = block
        half = block.shape[0] // 2
        for step in range(1, half_ring + 1):
            if step == half_ring:
                clock, counter = clock[:half], counter[half:]
            clock, counter = yield [(clock, go_next), (counter, go_prev)]
            found.append((clock, -step % n_g, 0))
            found.append((counter, step, half if step == half_ring else 0))
        lanes_left[name] -= 1

    def reduce_task(name, value, column):
        rows_of = value.shape[1]

        def mine(offset):
            return lax.dynamic_slice(value, (g_at(offset), 0, column), (1, rows_of, lane))[0]

        block = mine(half_ring)
        half = rows_of // 2
        clock, counter = block[:half], block[half:]
        for step in range(half_ring - 1, -1, -1):
            clock, counter = yield [(clock, go_next), (counter, go_prev)]
            clock, counter = clock.astype(F32), counter.astype(F32)
            up, down = mine(step).astype(F32), mine(-step).astype(F32)
            if step == half_ring - 1:
                clock = jnp.concatenate([up[:half] + clock, up[half:]]).astype(BF16)
                counter = jnp.concatenate([down[:half], down[half:] + counter]).astype(BF16)
            elif step:
                clock, counter = (up + clock).astype(BF16), (down + counter).astype(BF16)
        sums[name] = up + clock + counter

    waiting = [[], []]
    flying = [None, None]
    turn = 0

    def launch(side):
        if waiting[side] and flying[side] is None:
            task, rounds, sends = waiting[side].pop(0)
            if sends is None:
                sends = next(task)
            else:
                values = pin(*[value for value, pairs in sends])
                values = values if len(sends) > 1 else [values]
                sends = [(value, pairs) for value, (old, pairs) in zip(values, sends)]
            flying[side] = (task, rounds, [send(*item) for item in sends])

    def enter(side, task, rounds=0):
        waiting[side].append((task, rounds, None))
        launch(side)

    def visit(side):
        if flying[side] is None:
            return
        task, rounds, flight = flying[side]
        values = pin(*flight)
        flying[side] = None
        try:
            sends = task.send(values)
            if rounds == 1:
                waiting[side].append((task, 0, sends))
            else:
                flying[side] = (task, rounds - 1, [send(*item) for item in sends])
        except StopIteration:
            pass
        launch(side)

    def ring(steps):
        nonlocal turn
        for unused in range(steps):
            visit(turn)
            turn ^= 1

    def settle(name, shapes, moves):
        while lanes_left[name]:
            ring(1)
        plan = []
        values = []
        for side in range(2):
            for value, place, low in pieces[name, side]:
                high = low + value.shape[0]
                inside = []
                for (row, size), columns, out, (to_row, unused), to_columns in moves[side]:
                    first, last = max(row, low), min(row + size, high)
                    if first < last:
                        to = (to_row + first - row, last - first)
                        inside.append(((first - low, last - first), columns, out, to, to_columns))
                plan.append((len(values), place, inside))
                values.append(value)
        shapes = [(n_g,) + shape for shape in shapes]
        outs = assemble(plan, places, values, shapes)
        return [out.reshape(n_g * out.shape[1], out.shape[2]) for out in outs]

    def summed(name):
        while name not in sums:
            ring(1)
        return sums[name]

    def join_near(value, from_core):
        return jnp.concatenate([value, from_core])

    def send_far(far):
        from_diagonal = pin(send(far[1], swap_core))
        across = pin((far[0].astype(F32) + from_diagonal.astype(F32)).astype(BF16))
        return send(across, swap_x)

    def add_near(near, from_core, from_x):
        return near + from_x.astype(F32) + from_core.astype(F32)

    def pair(value):
        return value.reshape((2, value.shape[0] // 2) + value.shape[1:])

    to_ranks = []
    for i in range(n):
        head, part = i // parts, i % parts
        to_ranks.append((i, ((head // 4) * parts + part) * 4 + (head % 2) * 2 + (head // 2) % 2))
    from_ranks = [(j, i) for i, j in to_ranks]

    block_rows = 4 * own_rows
    block = (0, block_rows)
    stacked = [
        ((part * own_rows, own_rows), (rank_width, rank_width), 1, (0, own_rows), (part * rank_width, rank_width))
        for part in range(4)
    ]

    for side in range(2):
        enter(side, gather_task("down", side, mlp_out[:, side * lane : (side + 1) * lane]), 1)
    qkv_state = exchange_x(cut_columns([attn_query, attn_key, attn_value], head_cut))
    vectors = jnp.stack(
        [
            mask_embed,
            gain_attn,
            bias_attn,
            gain_cross,
            bias_cross,
            gain_mlp,
            bias_mlp,
            jnp.zeros_like(bias_mlp),
        ]
    ).astype(F32)[None]

    bits = n.bit_length() - 1
    later = [None, None]
    out_block = send(attn_out, to_ranks)
    for bit in range(bits):
        other = pin(send(vectors, [(i, i ^ (1 << bit)) for i in range(n)]))
        upper = (me >> bit) & 1 == 1
        vectors = jnp.concatenate(
            [jnp.where(upper, other, vectors), jnp.where(upper, vectors, other)]
        )
        if bit == 1:
            qkv_state = exchange_core(qkv_state)
        if bit == 2:
            qkv_lanes = in_order(qkv_state, pin(out_block))
            for side in range(2):
                enter(side, gather_task("self", side, qkv_lanes[side]))
                visit(side)
                later[side] = waiting[side].pop(0)
    whole_vectors = vectors.transpose(1, 0, 2).reshape(8, width)
    embed, g_attn, b_attn, g_cross, b_cross, g_mlp, b_mlp = [whole_vectors[k] for k in range(7)]

    masked = mask_flags[:, None] == 1
    start = jnp.where(masked, embed[None, :], tokens_in.astype(F32))
    unit_one, inverse_one = normalize(start)
    normed_one = pin((unit_one * g_attn + b_attn).astype(BF16))
    from_x = send(normed_one, swap_x)
    from_core = send(normed_one, swap_core)
    cross_blocks = pin(*cut_columns([cross_key, cross_value, cross_query], head_cut))
    one_near = join_near(normed_one, pin(from_core))
    ring(2)
    from_x = pin(from_x)
    cross_state = exchange_x(cross_blocks)
    one_far = jnp.concatenate([from_x, pin(send(from_x, swap_core))])
    cross_out_block = send(cross_out, to_ranks)
    ring(1)
    cross_state = exchange_core(cross_state)
    ring(1)
    half_text = jnp.stack(
        [
            jnp.where(x == 1, text_states[1], text_states[0]),
            jnp.where(x == 1, text_states[0], text_states[1]),
        ]
    )
    half_text, cross_out_block = pin(half_text, cross_out_block)
    text_x = send(half_text, swap_x)
    text_core = send(half_text, swap_core)
    cross_lanes = in_order(cross_state, cross_out_block)
    for side in range(2):
        enter(side, gather_task("cross", side, cross_lanes[side]))
    in_blocks = pin(*cut_columns([mlp_in], hidden_cut))
    ring(1)
    text_x, text_core = pin(text_x, text_core)
    in_state = exchange_x(in_blocks)
    text_diagonal = pin(send(text_x, swap_core))
    ring(1)
    text_rows = pin(
        jnp.concatenate(
            [
                half_text[0],
                text_x[1],
                text_core[0],
                text_diagonal[1],
                half_text[1],
                text_x[0],
                text_core[1],
                text_diagonal[0],
            ]
        )
    )
    in_state = exchange_core(in_state)
    ring(1)
    back_x = send(out_grad, swap_x)
    back_core = send(out_grad, swap_core)
    in_lanes = in_order(in_state)
    for side in range(2):
        enter(side, gather_task("in", side, in_lanes[side]))
        waiting[side].append(later[side])
    ring(1)

    pair_rows = 2 * rows
    score_flops = 2 * 2 * images * rank_heads * L * DH

    def self_forward(qkv):
        return by_image(
            functools.partial(self_forward_kernel, rank_width, scale),
            [qkv],
            [(L, 3 * rank_width)],
            [(pair_rows, rank_width)],
            [(L, rank_width)],
            2 * score_flops * L,
        )[0]

    def cross_forward(queries, text, skip):
        return by_image(
            functools.partial(cross_forward_kernel, rank_width, scale),
            [queries, text],
            [(L, rank_width), (ctx, 2 * rank_width)],
            [(pair_rows, rank_width)],
            [(L, rank_width)],
            2 * score_flops * ctx,
            skip,
        )[0]

    w_qkv, w_out = settle(
        "self",
        [(block_rows, 3 * rank_width), (own_rows, width)],
        [
            [(block, (0, lane), 0, block, (0, lane))],
            [(block, (0, rank_width), 0, block, (lane, rank_width))] + stacked,
        ],
    )
    qkv_far = pin(product(one_far, w_qkv).astype(BF16))
    mixed_far = self_forward(qkv_far)
    out_far = pin(product(mixed_far, w_out).astype(BF16))
    from_x = send_far(pair(out_far))
    ring(2)
    qkv_near = pin(product(one_near, w_qkv).astype(BF16))
    mixed_near = self_forward(qkv_near)
    out_near = pair(pin(product(mixed_near, w_out)))
    from_core = pin(send(out_near[1].astype(BF16), swap_core))
    back_x, back_core = pin(back_x, back_core)
    back_near = join_near(out_grad, back_core)
    back_far = jnp.concatenate([back_x, send(back_x, swap_core)])
    ring(2)
    first = start + add_near(out_near[0], from_core, pin(from_x))

    unit_two, inverse_two = normalize(first)
    first, normed_two = pin(first, (unit_two * g_cross + b_cross).astype(BF16))
    from_x = send(normed_two, swap_x)
    two_near = join_near(normed_two, pin(send(normed_two, swap_core)))
    ring(2)
    from_x = pin(from_x)
    two_far = jnp.concatenate([from_x, pin(send(from_x, swap_core))])
    ring(2)
    w_text, w_cross_out, w_cross = settle(
        "cross",
        [(block_rows, lane), (own_rows, width), (block_rows, rank_width)],
        [
            [(block, (0, lane), 0, block, (0, lane))],
            [(block, (0, rank_width), 2, block, (0, rank_width))] + stacked,
        ],
    )
    text_kv = pin(product(text_rows, w_text).astype(BF16))
    cross_far = product(two_far, w_cross).astype(BF16)
    cmixed_far = cross_forward(cross_far, text_kv, 2 * images)
    out_far = pin(product(cmixed_far, w_cross_out).astype(BF16))
    from_x = send_far(pair(out_far))
    ring(1)
    cross_near = product(two_near, w_cross).astype(BF16)
    cmixed_near = cross_forward(cross_near, text_kv, 0)
    out_near = pair(pin(product(cmixed_near, w_cross_out)))
    from_core = pin(send(out_near[1].astype(BF16), swap_core))
    ring(1)
    second = first + add_near(out_near[0], from_core, pin(from_x))

    unit_three, inverse_three = normalize(second)
    second, normed_three = pin(second, (unit_three * g_mlp + b_mlp).astype(BF16))
    from_x = send(normed_three, swap_x)
    three_near = join_near(normed_three, pin(send(normed_three, swap_core)))
    ring(2)
    from_x = pin(from_x)
    three_far = jnp.concatenate([from_x, pin(send(from_x, swap_core))])
    three_all = jnp.concatenate([three_near, three_far])
    ring(2)
    ring(2)
    (w_in,) = settle(
        "in",
        [(block_rows, width)],
        [[(block, (0, lane), 0, block, (side * lane, lane))] for side in range(2)],
    )

    def feed(values):
        hidden_pre = product(values, w_in)
        share = 0.5 + 0.5 * lax.erf(hidden_pre * (0.5**0.5))
        bell = jnp.exp(-0.5 * hidden_pre * hidden_pre) * 0.3989422804014327
        return pin((hidden_pre * share).astype(BF16), share + hidden_pre * bell)

    activated_near, slope_near = feed(three_near)
    ring(1)
    activated_far, slope_far = feed(three_far)
    ring(1)
    activated = jnp.concatenate([activated_near, activated_far])
    back_all = jnp.concatenate([back_near, back_far])
    down_part = pin(outer_grad(activated, back_all).astype(BF16)).reshape(n_g, hidden_rows, width)
    ring(2)
    for side in range(2):
        enter(side, reduce_task(("down", side), down_part, side * lane))
    ring(2)

    down_block = (0, hidden_rows)
    (w_down,) = settle(
        "down",
        [(hidden_rows, width)],
        [[(down_block, (0, lane), 0, down_block, (side * lane, lane))] for side in range(2)],
    )
    hidden_far = pin((back_project(back_far, w_down) * slope_far).astype(BF16))
    ring(1)
    three_grad = pin(back_project(hidden_far, w_in).astype(BF16))
    from_x = send_far(pair(three_grad))
    ring(1)
    hidden_near = pin((back_project(back_near, w_down) * slope_near).astype(BF16))
    three_grad = pair(pin(back_project(hidden_near, w_in)))
    from_core = pin(send(three_grad[1].astype(BF16), swap_core))
    ring(2)
    normed_three_grad = add_near(three_grad[0], from_core, pin(from_x))
    rows_three, gain_mlp_term, bias_mlp_term = norm_backward(
        normed_three_grad, unit_three, inverse_three, g_mlp
    )
    second_grad = out_grad.astype(F32) + rows_three
    second_grad, gain_mlp_term, bias_mlp_term, second_low = pin(
        second_grad, gain_mlp_term, bias_mlp_term, second_grad.astype(BF16)
    )
    from_x = send(second_low, swap_x)
    second_near = join_near(second_low, pin(send(second_low, swap_core)))
    hidden_all = jnp.concatenate([hidden_near, hidden_far])
    in_part = pin(outer_grad(three_all, hidden_all).astype(BF16))
    in_part = in_part.reshape(n_g, block_rows, hidden // 4)
    for side in range(2):
        enter(side, reduce_task(("in", side), in_part, side * lane))
    ring(2)

    def by_target(total):
        def rows_of(rel):
            low = (rank[0] ^ rel) * own_rows
            return lax.dynamic_slice(total, (low, 0), (own_rows, total.shape[1])).astype(BF16)

        return (rows_of(0), jnp.stack([rows_of(1), rows_of(3)]), rows_of(2))

    def stack_rows(part):
        cut = part.reshape(n_g, own_rows, width)
        size = width // 4
        return jnp.concatenate([cut[:, :, k * size : (k + 1) * size] for k in range(4)], axis=1)

    def unstack_rows(total):
        return jnp.concatenate(
            [total[k * own_rows : (k + 1) * own_rows] for k in range(4)], axis=1
        ).astype(BF16)

    def cross_backward(queries, text, grads, skip):
        return by_image(
            functools.partial(cross_backward_kernel, rank_width, scale),
            [queries, text, grads],
            [(L, rank_width), (ctx, 2 * rank_width), (L, rank_width)],
            [(pair_rows, rank_width), (2 * images * ctx, 2 * rank_width)],
            [(L, rank_width), (ctx, 2 * rank_width)],
            5 * score_flops * ctx,
            skip,
        )

    from_x = pin(from_x)
    second_far = jnp.concatenate([from_x, pin(send(from_x, swap_core))])
    cgrad_far = back_project(second_far, w_cross_out).astype(BF16)
    cq_far, tkv_far = cross_backward(cross_far, text_kv, cgrad_far, 2 * images)
    two_grad = pin(back_project(cq_far, w_cross).astype(BF16))
    from_x = send_far(pair(two_grad))
    ring(2)
    cgrad_near = back_project(second_near, w_cross_out).astype(BF16)
    cq_near, tkv_near = cross_backward(cross_near, text_kv, cgrad_near, 0)
    two_grad = pair(pin(back_project(cq_near, w_cross)))
    from_core = pin(send(two_grad[1].astype(BF16), swap_core))
    cmixed_all = jnp.concatenate([cmixed_near, cmixed_far])
    second_all = jnp.concatenate([second_near, second_far])
    cross_out_part = pin(outer_grad(cmixed_all, second_all).astype(BF16))
    ring(2)
    normed_two_grad = add_near(two_grad[0], from_core, pin(from_x))
    rows_two, gain_cross_term, bias_cross_term = norm_backward(
        normed_two_grad, unit_two, inverse_two, g_cross
    )
    first_grad = second_grad + rows_two
    first_grad, gain_cross_term, bias_cross_term, first_low = pin(
        first_grad, gain_cross_term, bias_cross_term, first_grad.astype(BF16)
    )
    from_x = send(first_low, swap_x)
    first_near = join_near(first_low, pin(send(first_low, swap_core)))
    two_all = jnp.concatenate([two_near, two_far])
    cq_all = jnp.concatenate([cq_near, cq_far])
    tkv_all = jnp.concatenate([tkv_near, tkv_far])
    cross_part = pin(outer_grad(two_all, cq_all).astype(BF16))
    ring(1)
    text_kv_part = pin(outer_grad(text_rows, tkv_all).astype(BF16))
    text_kv_part = text_kv_part.reshape(n_g, block_rows, lane)
    cross_part = cross_part.reshape(n_g, block_rows, rank_width)
    cross_part = jnp.concatenate([cross_part, stack_rows(cross_out_part)], axis=2)
    enter(0, reduce_task(("cross", 0), text_kv_part, 0))
    enter(1, reduce_task(("cross", 1), cross_part, 0))
    ring(1)
    sgrad_near = pin(back_project(first_near, w_out).astype(BF16))

    def self_backward(qkv, grads):
        return by_image(
            functools.partial(self_backward_kernel, rank_width, scale),
            [qkv, grads],
            [(L, 3 * rank_width), (L, rank_width)],
            [(pair_rows, 3 * rank_width)],
            [(L, 3 * rank_width)],
            5 * score_flops * L,
        )[0]

    qkv_grad_near = pin(self_backward(qkv_near, sgrad_near))
    from_x = pin(from_x)
    first_far = jnp.concatenate([from_x, pin(send(from_x, swap_core))])
    ring(2)
    sgrad_far = back_project(first_far, w_out).astype(BF16)
    qkv_grad_far = self_backward(qkv_far, sgrad_far)
    one_grad = pin(back_project(qkv_grad_far, w_qkv).astype(BF16))
    from_x = send_far(pair(one_grad))
    ring(1)
    one_all = jnp.concatenate([one_near, one_far])
    qkv_grad_all = jnp.concatenate([qkv_grad_near, qkv_grad_far])
    qkv_part = pin(outer_grad(one_all, qkv_grad_all).astype(BF16))
    ring(1)
    mixed_all = jnp.concatenate([mixed_near, mixed_far])
    first_all = jnp.concatenate([first_near, first_far])
    out_part = pin(outer_grad(mixed_all, first_all).astype(BF16))
    qkv_part = qkv_part.reshape(n_g, block_rows, 3 * rank_width)
    enter(0, reduce_task(("self", 0), qkv_part, 0))
    last_part = jnp.concatenate([qkv_part[:, :, lane:], stack_rows(out_part)], axis=2)
    enter(1, reduce_task(("self", 1), last_part, 0))
    ring(1)
    one_grad = pair(pin(back_project(qkv_grad_near, w_qkv)))
    from_core = pin(send(one_grad[1].astype(BF16), swap_core))
    ring(1)
    normed_one_grad = add_near(one_grad[0], from_core, pin(from_x))
    rows_one, gain_attn_term, bias_attn_term = norm_backward(
        normed_one_grad, unit_one, inverse_one, g_attn
    )
    start_grad = first_grad + rows_one
    tokens_grad = jnp.where(masked, 0.0, start_grad)
    embed_term = jnp.sum(jnp.where(masked, start_grad, 0.0), axis=0)
    tokens_grad, embed_term, gain_attn_term, bias_attn_term = pin(
        tokens_grad, embed_term, gain_attn_term, bias_attn_term
    )

    result_far = pin(product(activated_far, w_down).astype(BF16))
    ring(1)
    from_x = send_far(pair(result_far))
    result_near = pair(pin(product(activated_near, w_down)))
    from_core = pin(send(result_near[1].astype(BF16), swap_core))
    ring(2)
    text_part = pin(back_project(tkv_all, w_text)).reshape(8, ctx // 2, width)
    output = pin((second + add_near(result_near[0], from_core, pin(from_x))).astype(BF16))
    text_own = jnp.stack([text_part[0], text_part[4]])
    text_far = [
        jnp.stack([text_part[a], text_part[b]]).astype(BF16) for a, b in ((5, 1), (2, 6), (7, 3))
    ]
    from_x = send_far([text_far[0], text_far[2]])
    from_core = pin(send(text_far[1], swap_core))
    ring(2)
    text_sum = add_near(text_own, from_core, pin(from_x))
    text_grad = pin(
        jnp.stack(
            [
                jnp.where(x == 1, text_sum[1], text_sum[0]),
                jnp.where(x == 1, text_sum[0], text_sum[1]),
            ]
        )
    )
    in_sum = jnp.concatenate([summed(("in", 0)), summed(("in", 1))], axis=1)
    in_state = exchange_core(exchange_x(by_target(in_sum)))
    ring(2)
    (mlp_in_grad,) = join_columns(*exchange_end(in_state), hidden_cut, 1)
    mlp_in_grad = pin(mlp_in_grad)
    mlp_out_grad = pin(jnp.concatenate([summed(("down", 0)), summed(("down", 1))], axis=1))

    terms = jnp.stack(
        [
            embed_term,
            gain_attn_term,
            bias_attn_term,
            gain_cross_term,
            bias_cross_term,
            gain_mlp_term,
            bias_mlp_term,
            jnp.zeros_like(bias_mlp_term),
        ]
    )
    terms = terms.reshape(8, n, own_rows).transpose(1, 0, 2)
    for bit in reversed(range(bits)):
        upper = (me >> bit) & 1 == 1
        count = terms.shape[0] // 2
        keep = jnp.where(upper, terms[count:], terms[:count])
        away = jnp.where(upper, terms[:count], terms[count:])
        terms = keep + pin(send(away, [(i, i ^ (1 << bit)) for i in range(n)]))
    terms = terms[0]

    text_kv_sum = summed(("cross", 0))
    cross_sum = summed(("cross", 1))
    cross_total = jnp.concatenate([text_kv_sum, cross_sum[:, :rank_width]], axis=1)
    cross_state = exchange_x(by_target(cross_total))
    cross_out_grad = send(unstack_rows(cross_sum[:, rank_width:]), from_ranks)
    ring(1)
    cross_state = exchange_core(cross_state)
    ring(1)
    cross_key_grad, cross_value_grad, cross_query_grad = join_columns(
        *exchange_end(cross_state), head_cut, 3
    )
    cross_query_grad, cross_key_grad, cross_value_grad, cross_out_grad = pin(
        cross_query_grad, cross_key_grad, cross_value_grad, cross_out_grad.astype(F32)
    )
    qkv_sum = summed(("self", 0))
    last_sum = summed(("self", 1))
    qkv_sum = jnp.concatenate([qkv_sum, last_sum[:, :rank_width]], axis=1)
    attn_out_grad = send(unstack_rows(last_sum[:, rank_width:]), from_ranks).astype(F32)
    qkv_state = exchange_core(exchange_x(by_target(qkv_sum)))
    attn_query_grad, attn_key_grad, attn_value_grad = join_columns(
        *exchange_end(qkv_state), head_cut, 3
    )

    return (
        output,
        tokens_grad,
        text_grad,
        terms[0],
        terms[1],
        terms[2],
        attn_query_grad,
        attn_key_grad,
        attn_value_grad,
        attn_out_grad,
        terms[3],
        terms[4],
        cross_query_grad,
        cross_key_grad,
        cross_value_grad,
        cross_out_grad,
        terms[5],
        terms[6],
        mlp_in_grad,
        mlp_out_grad,
    )


def solution(mesh):
    devices = mesh.devices.reshape(mesh.shape["dp"] // 2, 2, mesh.shape["text"])
    groups = jax.sharding.Mesh(devices, ("g", "core", "x"))
    spec_rows = P(AXES, None)
    spec_text = P(("g", "core"), "x", None)
    spec_vector = P(AXES)
    return jax.shard_map(
        functools.partial(on_device, groups.shape["g"]),
        mesh=groups,
        in_specs=(spec_rows, spec_vector, spec_text)
        + (spec_vector,) * 3
        + (spec_rows,) * 4
        + (spec_vector,) * 2
        + (spec_rows,) * 4
        + (spec_vector,) * 2
        + (spec_rows,) * 3,
        out_specs=(spec_rows, spec_rows, spec_text)
        + (spec_vector,) * 3
        + (spec_rows,) * 4
        + (spec_vector,) * 2
        + (spec_rows,) * 4
        + (spec_vector,) * 2
        + (spec_rows,) * 2,
        check_vma=False,
    )
```

time: 6850 us -> 1040 us (0.15)
  waiting for transfers between devices: 6270 us -> 448 us
  starting transfers between devices: 9.55 us -> 221 us
  matrix products: 329 us -> 164 us
  blocking collectives: 117 us -> 0 us
    reduce_scatter x8 -> x0, waiting for transfers between devices: 4660 us -> none  [the longest x1 1410 us: on_device(): lax.psum_scatter(mlp_in_full, ('dp', 'text'), scatter_dimension=0, tiled=...]
    all_gather x10 -> x0, waiting for transfers between devices: 877 us -> none  [the longest x1 189 us: on_device(): lax.all_gather(mlp_in, ('dp', 'text'), axis=0, tiled=True)]
    unnamed x22 -> x0, waiting for transfers between devices: 729 us -> none
    ppermute x0 -> x196, waiting for transfers between devices: none -> 448 us  [send(): return lax.ppermute(value, AXES, pairs)]
    ppermute x0 -> x196, starting transfers between devices: none -> 221 us  [send(): return lax.ppermute(value, AXES, pairs)]
    unnamed x2 -> x0, blocking collectives: 83.6 us -> none
  transfers between devices with their start and end apart: 22 -> 196, of which waited for: 21 -> 87; matrix products, arithmetic and copies ran while one was open for 5% -> 22% of each run, Pallas kernels for 0% -> 3%
where the time goes in v1:
time: 1040 us; the launch traced here: 1030 us
  waiting for transfers between devices  448 us (43%)
  starting transfers between devices  221 us (21%)
  matrix products  164 us (16%)
  other arithmetic  85.7 us (8%)
  local copies, waits for them, and re-layouts  67.7 us (7%)
  Pallas kernels  41.6 us (4%)
    ppermute x196, waiting for transfers between devices, send(): return lax.ppermute(value, AXES, pairs)  448 us
    ppermute x196, starting transfers between devices, send(): return lax.ppermute(value, AXES, pairs)  221 us
    dot_general x13, matrix products, back_project(): lax.dot_general(left, right, (((1,), (1,)), ((), ())), preferred_element_...  58.3 us
    dot_general x7, matrix products, outer_grad(): lax.dot_general(left, right, (((0,), (0,)), ((), ())), preferred_element_...  52.7 us
    dot_general x13, matrix products, product(): return jnp.dot(left, right, preferred_element_type=F32)  52.6 us
    unnamed x492, local copies, waits for them, and re-layouts  37.8 us
    pallas_call x8, Pallas kernels, by_image(): pl.pallas_call(kernel, grid=(images,), in_specs=[pl.BlockSpec(block, func...  23.5 us
    convert_element_type x12, other arithmetic, reduce_task(): clock, counter = ((up + clock).astype(BF16), (down + counter).astype(BF16))  22 us
  transfers between devices with their start and end apart: 196, of which 87 were waited for; matrix products, arithmetic and copies ran while one was open for 22% of the time, Pallas kernels for 3%

profile of v1, /device:TPU:3, one launch (start us, length us, event | category | flops | bytes accessed | tf_op | source)
XLA Modules:
  0.0 1031.6 jit_solution(9368427396174563993)
XLA Ops:
  31.8 15.3 %collective-permute-done.7.refs_1_ = bf16[256,1024]{1,0:T(8,128)(2,1)S(1)} collective-permute-done((bf16[256,1024]{1,0:T(8,128)(2,1)S(1)}, bf16[256,1024]{1,0:T(8,128)(2,1)S(1)}, u32[]{:S(2)}, u32[]{:S(2)}) %collective-permute-start.7) | collective-permute-done | bytes 524320 | tf_op jit(solution)/shard_map/ppermute | solution.py:265
  101.0 12.7 %collective-permute-done.15.refs_3_ = bf16[256,1024]{1,0:T(8,128)(2,1)} collective-permute-done((bf16[256,1024]{1,0:T(8,128)(2,1)S(1)}, bf16[256,1024]{1,0:T(8,128)(2,1)}, u32[]{:S(2)}, u32[]{:S(2)}) %collective-permute-start.15) | collective-permute-done | bytes 524320 | tf_op jit(solution)/shard_map/ppermute | solution.py:265
  116.4 10.0 collective-permute-done.26.refs_12_
  208.9 15.6 %collective-permute-done.41.refs_1_ = bf16[256,1024]{1,0:T(8,128)(2,1)S(1)} collective-permute-done((bf16[256,1024]{1,0:T(8,128)(2,1)S(1)}, bf16[256,1024]{1,0:T(8,128)(2,1)S(1)}, u32[]{:S(2)}, u32[]{:S(2)}) %collective-permute-start.41) | collective-permute-done | bytes 524320 | tf_op jit(solution)/shard_map/ppermute | solution.py:265
  245.8 10.8 %collective-permute-done.45.refs_12_ = bf16[256,1024]{1,0:T(8,128)(2,1)} collective-permute-done((bf16[256,1024]{1,0:T(8,128)(2,1)S(1)}, bf16[256,1024]{1,0:T(8,128)(2,1)}, u32[]{:S(2)}, u32[]{:S(2)}) %collective-permute-start.45) | collective-permute-done | bytes 524320 | tf_op jit(solution)/shard_map/ppermute | solution.py:265
  267.0 10.4 %collective-permute-done.53.refs_5_ = bf16[256,1024]{1,0:T(8,128)(2,1)S(1)} collective-permute-done((bf16[256,1024]{1,0:T(8,128)(2,1)}, bf16[256,1024]{1,0:T(8,128)(2,1)S(1)}, u32[]{:S(2)}, u32[]{:S(2)}) %collective-permute-start.53) | collective-permute-done | bytes 524320 | tf_op jit(solution)/shard_map/ppermute | solution.py:265
  278.4 10.2 collective-permute-done.58.refs_14_
  335.8 11.4 %collective-permute-done.67.refs_10_ = bf16[256,1024]{1,0:T(8,128)(2,1)} collective-permute-done((bf16[256,1024]{1,0:T(8,128)(2,1)}, bf16[256,1024]{1,0:T(8,128)(2,1)}, u32[]{:S(2)}, u32[]{:S(2)}) %collective-permute-start.67) | collective-permute-done | bytes 524320 | tf_op jit(solution)/shard_map/ppermute | solution.py:265
  347.8 10.4 %collective-permute-done.66 = bf16[256,2048]{1,0:T(8,128)(2,1)} collective-permute-done((bf16[256,2048]{1,0:T(8,128)(2,1)}, bf16[256,2048]{1,0:T(8,128)(2,1)}, u32[]{:S(2)}, u32[]{:S(2)}) %collective-permute-start.66) | collective-permute-done | bytes 1048608 | tf_op jit(solution)/shard_map/ppermute | solution.py:265
  367.3 10.2 collective-permute-done.71.refs_3_
  378.0 10.8 %collective-permute-done.76.refs_12_ = bf16[256,1024]{1,0:T(8,128)(2,1)S(1)} collective-permute-done((bf16[256,1024]{1,0:T(8,128)(2,1)}, bf16[256,1024]{1,0:T(8,128)(2,1)S(1)}, u32[]{:S(2)}, u32[]{:S(2)}) %collective-permute-start.76) | collective-permute-done | bytes 524320 | tf_op jit(solution)/shard_map/ppermute | solution.py:265
  393.6 10.6 %collective-permute-done.73.refs_5_ = bf16[256,1024]{1,0:T(8,128)(2,1)S(1)} collective-permute-done((bf16[256,1024]{1,0:T(8,128)(2,1)S(1)}, bf16[256,1024]{1,0:T(8,128)(2,1)S(1)}, u32[]{:S(2)}, u32[]{:S(2)}) %collective-permute-start.73) | collective-permute-done | bytes 524320 | tf_op jit(solution)/shard_map/ppermute | solution.py:265
  453.0 13.3 %convolution_convert_fusion.2 = bf16[2048,2048]{1,0:T(8,128)(2,1)} fusion(bf16[512,2048]{1,0:T(8,128)(2,1)} %get-tuple-element.694, bf16[512,2048]{1,0:T(8,128)(2,1)S(1)} %get-tuple-element.686, bf16[256,2048]{1,0:T(8,128)(2,1)S(1)} %collective-permute-done.89, bf16[256,2048]{1,0:T(8,128)(2,1)S(1)} %copy-done.214, bf16[256,2048]{1,0:T(8,128)(2,1)S(1)} %copy-done.216, ...), kind=kOutput, calls=%fused_computation.2 | convolution fusion | flops 8619294720 | bytes 16777216 | tf_op jit(solution)/shard_map/dot_general | solution.py:38
  492.7 11.1 %multiply_convert_fusion = bf16[512,2048]{1,0:T(8,128)(2,1)} fusion(f32[512,2048]{1,0:T(8,128)} %get-tuple-element.717, bf16[2048,2048]{1,0:T(8,128)(2,1)S(1)} %bitcast.406, bf16[256,2048]{1,0:T(8,128)(2,1)} %copy-done.223, bf16[256,2048]{1,0:T(8,128)(2,1)} %copy-done.213), kind=kOutput, calls=%fused_computation.66 | convolution fusion | flops 4301258752 | bytes 16777216 | tf_op jit(solution)/shard_map/dot_general | solution.py:42
  547.3 9.8 fusion.264
  557.2 10.7 %collective-permute-done.106 = bf16[256,1024]{1,0:T(8,128)(2,1)S(1)} collective-permute-done((bf16[256,1024]{1,0:T(8,128)(2,1)S(1)}, bf16[256,1024]{1,0:T(8,128)(2,1)S(1)}, u32[]{:S(2)}, u32[]{:S(2)}) %collective-permute-start.106) | collective-permute-done | bytes 524320 | tf_op jit(solution)/shard_map/ppermute | solution.py:265
  589.7 11.4 %convolution_convert_fusion.1 = bf16[2048,2048]{1,0:T(8,128)(2,1)} fusion(bf16[256,2048]{1,0:T(8,128)(2,1)S(1)} %copy-done.222, bf16[256,2048]{1,0:T(8,128)(2,1)S(1)} %copy-done.220, bf16[256,2048]{1,0:T(8,128)(2,1)S(1)} %copy-done.218, bf16[256,2048]{1,0:T(8,128)(2,1)S(1)} %copy-done.148, bf16[512,2048]{1,0:T(8,128)(2,1)S(1)} %copy-done.228, ...), kind=kOutput, calls=%fused_computation.1 | convolution fusion | flops 8619294720 | bytes 16777216 | tf_op jit(solution)/shard_map/dot_general | solution.py:38
  654.7 10.9 %collective-permute-done.117 = bf16[256,1024]{1,0:T(8,128)(2,1)S(1)} collective-permute-done((bf16[256,1024]{1,0:T(8,128)(2,1)S(1)}, bf16[256,1024]{1,0:T(8,128)(2,1)S(1)}, u32[]{:S(2)}, u32[]{:S(2)}) %collective-permute-start.117) | collective-permute-done | bytes 524320 | tf_op jit(solution)/shard_map/ppermute | solution.py:265
  688.3 15.9 %collective-permute-done.121 = bf16[256,2048]{1,0:T(8,128)(2,1)S(1)} collective-permute-done((bf16[256,2048]{1,0:T(8,128)(2,1)S(1)}, bf16[256,2048]{1,0:T(8,128)(2,1)S(1)}, u32[]{:S(2)}, u32[]{:S(2)}) %collective-permute-start.121) | collective-permute-done | bytes 1048608 | tf_op jit(solution)/shard_map/ppermute | solution.py:265
  722.3 15.9 %collective-permute-done.130 = bf16[256,1024]{1,0:T(8,128)(2,1)} collective-permute-done((bf16[256,1024]{1,0:T(8,128)(2,1)}, bf16[256,1024]{1,0:T(8,128)(2,1)}, u32[]{:S(2)}, u32[]{:S(2)}) %collective-permute-start.130) | collective-permute-done | bytes 524320 | tf_op jit(solution)/shard_map/ppermute | solution.py:265
  776.5 10.2 convolution_convert_fusion
  800.8 18.2 %collective-permute-done.142 = bf16[256,1024]{1,0:T(8,128)(2,1)S(1)} collective-permute-done((bf16[256,1024]{1,0:T(8,128)(2,1)S(1)}, bf16[256,1024]{1,0:T(8,128)(2,1)S(1)}, u32[]{:S(2)}, u32[]{:S(2)}) %collective-permute-start.142) | collective-permute-done | bytes 524320 | tf_op jit(solution)/shard_map/ppermute | solution.py:265
  819.9 11.5 %collective-permute-done.143 = bf16[256,1024]{1,0:T(8,128)(2,1)S(1)} collective-permute-done((bf16[256,1024]{1,0:T(8,128)(2,1)S(1)}, bf16[256,1024]{1,0:T(8,128)(2,1)S(1)}, u32[]{:S(2)}, u32[]{:S(2)}) %collective-permute-start.143) | collective-permute-done | bytes 524320 | tf_op jit(solution)/shard_map/ppermute | solution.py:265
  989.2 11.4 %collective-permute-done.192 = bf16[64,2048]{1,0:T(8,128)(2,1)S(1)} collective-permute-done((bf16[64,2048]{1,0:T(8,128)(2,1)S(1)}, bf16[64,2048]{1,0:T(8,128)(2,1)S(1)}, u32[]{:S(2)}, u32[]{:S(2)}) %collective-permute-start.192) | collective-permute-done | bytes 262176 | tf_op jit(solution)/shard_map/ppermute | solution.py:265
  (1115 shorter events, 738.3 us)
Async XLA Ops:
  199.6 33.3 %collective-permute-start.49 = (bf16[256,2048]{1,0:T(8,128)(2,1)S(1)}, bf16[256,2048]{1,0:T(8,128)(2,1)S(1)}, u32[]{:S(2)}, u32[]{:S(2)}) collective-permute-start(bf16[256,2048]{1,0:T(8,128)(2,1)S(1)} %copy-done.131), channel_id=1, source_target_pairs={{0,1},{1,0},{2,3},{3,2},{4,5},{5,4},{6,7},{7,6},{8,9},{9,8},{10,11... | collective-permute-start | bytes 3145736 | tf_op jit(solution)/shard_map/ppermute | solution.py:265
  417.9 35.1 %collective-permute-start.89 = (bf16[256,2048]{1,0:T(8,128)(2,1)S(1)}, bf16[256,2048]{1,0:T(8,128)(2,1)S(1)}, u32[]{:S(2)}, u32[]{:S(2)}) collective-permute-start(bf16[256,2048]{1,0:T(8,128)(2,1)S(1)} %copy-done.214), channel_id=1, source_target_pairs={{0,2},{1,3},{2,0},{3,1},{4,6},{5,7},{6,4},{7,5},{8,10},{9,11},{10,... | collective-permute-start | bytes 3145736 | tf_op jit(solution)/shard_map/ppermute | solution.py:265
  479.7 50.9 %collective-permute-start.98 = (bf16[128,1024]{1,0:T(8,128)(2,1)}, bf16[128,1024]{1,0:T(8,128)(2,1)}, u32[]{:S(2)}, u32[]{:S(2)}) collective-permute-start(bf16[128,1024]{1,0:T(8,128)(2,1)} %get-tuple-element.1011), channel_id=1, source_target_pairs={{0,8},{1,9},{2,10},{3,11},{4,0},{5,1},{6,2},{7,3},{8,16},{9,17},{1... | collective-permute-start | bytes 786440 | tf_op jit(solution)/shard_map/ppermute | solution.py:265
  480.2 50.5 %collective-permute-start.99 = (bf16[128,1024]{1,0:T(8,128)(2,1)}, bf16[128,1024]{1,0:T(8,128)(2,1)}, u32[]{:S(2)}, u32[]{:S(2)}) collective-permute-start(bf16[128,1024]{1,0:T(8,128)(2,1)} %get-tuple-element.1015), channel_id=1, source_target_pairs={{8,0},{9,1},{10,2},{11,3},{0,4},{1,5},{2,6},{3,7},{16,8},{17,9},{1... | collective-permute-start | bytes 786440 | tf_op jit(solution)/shard_map/ppermute | solution.py:265
  481.2 31.2 %collective-permute-start.100 = (bf16[128,1024]{1,0:T(8,128)(2,1)}, bf16[128,1024]{1,0:T(8,128)(2,1)S(1)}, u32[]{:S(2)}, u32[]{:S(2)}) collective-permute-start(bf16[128,1024]{1,0:T(8,128)(2,1)} %get-tuple-element.1010), channel_id=1, source_target_pairs={{0,8},{1,9},{2,10},{3,11},{4,0},{5,1},{6,2},{7,3},{8,16},{9,17},{1... | collective-permute-start | bytes 786440 | tf_op jit(solution)/shard_map/ppermute | solution.py:265
  581.7 34.3 %collective-permute-start.118 = (bf16[256,2048]{1,0:T(8,128)(2,1)}, bf16[256,2048]{1,0:T(8,128)(2,1)}, u32[]{:S(2)}, u32[]{:S(2)}) collective-permute-start(bf16[256,2048]{1,0:T(8,128)(2,1)} %get-tuple-element.744), channel_id=1, source_target_pairs={{0,1},{1,0},{2,3},{3,2},{4,5},{5,4},{6,7},{7,6},{8,9},{9,8},{10,11... | collective-permute-start | bytes 3145736 | tf_op jit(solution)/shard_map/ppermute | solution.py:265
  613.4 53.4 %collective-permute-start.114 = (bf16[256,1024]{1,0:T(8,128)(2,1)S(1)}, bf16[256,1024]{1,0:T(8,128)(2,1)S(1)}, u32[]{:S(2)}, u32[]{:S(2)}) collective-permute-start(bf16[256,1024]{1,0:T(8,128)(2,1)S(1)} %get-tuple-element.1003), channel_id=1, source_target_pairs={{0,8},{1,9},{2,10},{3,11},{4,0},{5,1},{6,2},{7,3},{8,16},{9,17},{1... | collective-permute-start | bytes 1572872 | tf_op jit(solution)/shard_map/ppermute | solution.py:265
  614.6 53.2 %collective-permute-start.115 = (bf16[256,1024]{1,0:T(8,128)(2,1)S(1)}, bf16[256,1024]{1,0:T(8,128)(2,1)S(1)}, u32[]{:S(2)}, u32[]{:S(2)}) collective-permute-start(bf16[256,1024]{1,0:T(8,128)(2,1)S(1)} %get-tuple-element.1002), channel_id=1, source_target_pairs={{8,0},{9,1},{10,2},{11,3},{0,4},{1,5},{2,6},{3,7},{16,8},{17,9},{1... | collective-permute-start | bytes 1572872 | tf_op jit(solution)/shard_map/ppermute | solution.py:265
  614.9 39.2 %collective-permute-start.116 = (bf16[256,1024]{1,0:T(8,128)(2,1)S(1)}, bf16[256,1024]{1,0:T(8,128)(2,1)S(1)}, u32[]{:S(2)}, u32[]{:S(2)}) collective-permute-start(bf16[256,1024]{1,0:T(8,128)(2,1)S(1)} %get-tuple-element.1001), channel_id=1, source_target_pairs={{0,8},{1,9},{2,10},{3,11},{4,0},{5,1},{6,2},{7,3},{8,16},{9,17},{1... | collective-permute-start | bytes 1572872 | tf_op jit(solution)/shard_map/ppermute | solution.py:265
  652.5 35.8 %collective-permute-start.122 = (bf16[128,1024]{1,0:T(8,128)(2,1)S(1)}, bf16[128,1024]{1,0:T(8,128)(2,1)S(1)}, u32[]{:S(2)}, u32[]{:S(2)}) collective-permute-start(bf16[128,1024]{1,0:T(8,128)(2,1)S(1)} %get-tuple-element.991), channel_id=1, source_target_pairs={{0,8},{1,9},{2,10},{3,11},{4,0},{5,1},{6,2},{7,3},{8,16},{9,17},{1... | collective-permute-start | bytes 786440 | tf_op jit(solution)/shard_map/ppermute | solution.py:265
  654.1 34.2 %collective-permute-start.123 = (bf16[128,1024]{1,0:T(8,128)(2,1)S(1)}, bf16[128,1024]{1,0:T(8,128)(2,1)S(1)}, u32[]{:S(2)}, u32[]{:S(2)}) collective-permute-start(bf16[128,1024]{1,0:T(8,128)(2,1)S(1)} %get-tuple-element.995), channel_id=1, source_target_pairs={{8,0},{9,1},{10,2},{11,3},{0,4},{1,5},{2,6},{3,7},{16,8},{17,9},{1... | collective-permute-start | bytes 786440 | tf_op jit(solution)/shard_map/ppermute | solution.py:265
  709.9 39.7 %collective-permute-start.134 = (bf16[256,2048]{1,0:T(8,128)(2,1)S(1)}, bf16[256,2048]{1,0:T(8,128)(2,1)}, u32[]{:S(2)}, u32[]{:S(2)}) collective-permute-start(bf16[256,2048]{1,0:T(8,128)(2,1)S(1)} %get-tuple-element.784), channel_id=1, source_target_pairs={{0,1},{1,0},{2,3},{3,2},{4,5},{5,4},{6,7},{7,6},{8,9},{9,8},{10,11... | collective-permute-start | bytes 3145736 | tf_op jit(solution)/shard_map/ppermute | solution.py:265
  748.2 86.1 %collective-permute-start.132 = (bf16[128,1024]{1,0:T(8,128)(2,1)}, bf16[128,1024]{1,0:T(8,128)(2,1)S(1)}, u32[]{:S(2)}, u32[]{:S(2)}) collective-permute-start(bf16[128,1024]{1,0:T(8,128)(2,1)} %get-tuple-element.1057), channel_id=1, source_target_pairs={{0,8},{1,9},{2,10},{3,11},{4,0},{5,1},{6,2},{7,3},{8,16},{9,17},{1... | collective-permute-start | bytes 786440 | tf_op jit(solution)/shard_map/ppermute | solution.py:265
  748.9 85.4 %collective-permute-start.133 = (bf16[128,1024]{1,0:T(8,128)(2,1)}, bf16[128,1024]{1,0:T(8,128)(2,1)}, u32[]{:S(2)}, u32[]{:S(2)}) collective-permute-start(bf16[128,1024]{1,0:T(8,128)(2,1)} %get-tuple-element.1059), channel_id=1, source_target_pairs={{8,0},{9,1},{10,2},{11,3},{0,4},{1,5},{2,6},{3,7},{16,8},{17,9},{1... | collective-permute-start | bytes 786440 | tf_op jit(solution)/shard_map/ppermute | solution.py:265
  794.3 37.1 %collective-permute-start.140 = (bf16[256,1024]{1,0:T(8,128)(2,1)S(1)}, bf16[256,1024]{1,0:T(8,128)(2,1)S(1)}, u32[]{:S(2)}, u32[]{:S(2)}) collective-permute-start(bf16[256,1024]{1,0:T(8,128)(2,1)S(1)} %get-tuple-element.983), channel_id=1, source_target_pairs={{0,8},{1,9},{2,10},{3,11},{4,0},{5,1},{6,2},{7,3},{8,16},{9,17},{1... | collective-permute-start | bytes 1572872 | tf_op jit(solution)/shard_map/ppermute | solution.py:265
  800.1 31.3 %collective-permute-start.141 = (bf16[256,1024]{1,0:T(8,128)(2,1)S(1)}, bf16[256,1024]{1,0:T(8,128)(2,1)S(1)}, u32[]{:S(2)}, u32[]{:S(2)}) collective-permute-start(bf16[256,1024]{1,0:T(8,128)(2,1)S(1)} %get-tuple-element.982), channel_id=1, source_target_pairs={{8,0},{9,1},{10,2},{11,3},{0,4},{1,5},{2,6},{3,7},{16,8},{17,9},{1... | collective-permute-start | bytes 1572872 | tf_op jit(solution)/shard_map/ppermute | solution.py:265
  835.8 42.7 %collective-permute-start.148 = (bf16[256,2048]{1,0:T(8,128)(2,1)S(1)}, bf16[256,2048]{1,0:T(8,128)(2,1)S(1)}, u32[]{:S(2)}, u32[]{:S(2)}) collective-permute-start(bf16[256,2048]{1,0:T(8,128)(2,1)S(1)} %slice.1167), channel_id=1, source_target_pairs={{0,2},{1,3},{2,0},{3,1},{4,6},{5,7},{6,4},{7,5},{8,10},{9,11},{10,... | collective-permute-start | bytes 3145736 | tf_op jit(solution)/shard_map/ppermute | solution.py:265
  852.5 31.1 %collective-permute-start.145 = (bf16[256,2048]{1,0:T(8,128)(2,1)S(1)}, bf16[256,2048]{1,0:T(8,128)(2,1)S(1)}, u32[]{:S(2)}, u32[]{:S(2)}) collective-permute-start(bf16[256,2048]{1,0:T(8,128)(2,1)S(1)} %add_convert_fusion.2), channel_id=1, source_target_pairs={{0,1},{1,0},{2,3},{3,2},{4,5},{5,4},{6,7},{7,6},{8,9},{9,8},{10,11... | collective-permute-start | bytes 3145736 | tf_op jit(solution)/shard_map/ppermute | solution.py:265
  876.9 32.8 %collective-permute-start.150 = (bf16[256,1024]{1,0:T(8,128)(2,1)}, bf16[256,1024]{1,0:T(8,128)(2,1)}, u32[]{:S(2)}, u32[]{:S(2)}) collective-permute-start(bf16[256,1024]{1,0:T(8,128)(2,1)} %pad_maximum_fusion.12), channel_id=1, source_target_pairs={{0,8},{1,9},{2,10},{3,11},{4,0},{5,1},{6,2},{7,3},{8,16},{9,17},{1... | collective-permute-start | bytes 1572872 | tf_op jit(solution)/shard_map/ppermute | solution.py:265
  878.5 37.4 %collective-permute-start.151 = (bf16[256,1024]{1,0:T(8,128)(2,1)}, bf16[256,1024]{1,0:T(8,128)(2,1)}, u32[]{:S(2)}, u32[]{:S(2)}) collective-permute-start(bf16[256,1024]{1,0:T(8,128)(2,1)} %pad_maximum_fusion.13), channel_id=1, source_target_pairs={{8,0},{9,1},{10,2},{11,3},{0,4},{1,5},{2,6},{3,7},{16,8},{17,9},{1... | collective-permute-start | bytes 1572872 | tf_op jit(solution)/shard_map/ppermute | solution.py:265
  879.7 36.3 %collective-permute-start.167 = (bf16[2,64,2048]{2,1,0:T(8,128)(2,1)}, bf16[2,64,2048]{2,1,0:T(8,128)(2,1)S(1)}, u32[]{:S(2)}, u32[]{:S(2)}) collective-permute-start(bf16[2,64,2048]{2,1,0:T(8,128)(2,1)} %pad_maximum_fusion.23), channel_id=1, source_target_pairs={{0,2},{1,3},{2,0},{3,1},{4,6},{5,7},{6,4},{7,5},{8,10},{9,11},{10,... | collective-permute-start | bytes 1572872 | tf_op jit(solution)/shard_map/ppermute | solution.py:265
  883.2 36.5 %collective-permute-start.186 = (bf16[256,1024]{1,0:T(8,128)(2,1)}, bf16[256,1024]{1,0:T(8,128)(2,1)}, u32[]{:S(2)}, u32[]{:S(2)}) collective-permute-start(bf16[256,1024]{1,0:T(8,128)(2,1)} %get-tuple-element.1047), channel_id=1, source_target_pairs={{0,8},{1,9},{2,10},{3,11},{4,0},{5,1},{6,2},{7,3},{8,16},{9,17},{1... | collective-permute-start | bytes 1572872 | tf_op jit(solution)/shard_map/ppermute | solution.py:265
  929.6 38.3 %collective-permute-start.155 = (bf16[256,1024]{1,0:T(8,128)(2,1)S(1)}, bf16[256,1024]{1,0:T(8,128)(2,1)S(1)}, u32[]{:S(2)}, u32[]{:S(2)}) collective-permute-start(bf16[256,1024]{1,0:T(8,128)(2,1)S(1)} %pad_maximum_fusion.14), channel_id=1, source_target_pairs={{0,8},{1,9},{2,10},{3,11},{4,0},{5,1},{6,2},{7,3},{8,16},{9,17},{1... | collective-permute-start | bytes 1572872 | tf_op jit(solution)/shard_map/ppermute | solution.py:265
  930.3 37.6 %collective-permute-start.156 = (bf16[256,1024]{1,0:T(8,128)(2,1)S(1)}, bf16[256,1024]{1,0:T(8,128)(2,1)S(1)}, u32[]{:S(2)}, u32[]{:S(2)}) collective-permute-start(bf16[256,1024]{1,0:T(8,128)(2,1)S(1)} %pad_maximum_fusion.15), channel_id=1, source_target_pairs={{8,0},{9,1},{10,2},{11,3},{0,4},{1,5},{2,6},{3,7},{16,8},{17,9},{1... | collective-permute-start | bytes 1572872 | tf_op jit(solution)/shard_map/ppermute | solution.py:265
  (414 other events, 6012.4 us)

commit v2 on v1

--- a/solution.py
+++ b/solution.py
@@ -148,35 +148,41 @@
 
 
 def order_kernel(rank_ref, own, from_x, from_core, *refs):
-    extra, (first, second) = refs[:-2], refs[-2:]
+    extra, out = refs[:-1], refs[-1]
     rows, columns = own.shape
-    lane = first.shape[1]
     for rel, source in ((0, own), (1, from_x.at[0]), (2, from_core.at[0]), (3, from_core.at[1])):
         at = pl.ds(pl.multiple_of((rank_ref[0] ^ rel) * rows, rows), rows)
-        first[at, :] = source[:, :lane]
-        second[at, : columns - lane] = source[:, lane:]
+        out[at, :columns] = source[...]
     for weight in extra:
         size = weight.shape[1] // 4
         for part in range(4):
             piece = weight[:, part * size : (part + 1) * size]
-            second[part * rows : (part + 1) * rows, columns - lane :] = piece
+            out[part * rows : (part + 1) * rows, columns:] = piece
 
 
 def assemble_kernel(plan, count, places_ref, *refs):
-    sources, outs, sems = refs[:count], refs[count:-1], refs[-1]
-    copies = []
-    for piece, place, moves in plan:
+    sources, refs = refs[:count], refs[count:]
+    outs, held, loaded, stored = refs[: -2 - count], refs[-2 - count : -2], refs[-2], refs[-1]
+    loads = [
+        pltpu.make_async_copy(source, buffer, loaded.at[k])
+        for k, (source, buffer) in enumerate(zip(sources, held))
+    ]
+    for load in loads:
+        load.start()
+    stores = []
+    for load, buffer, (place, moves) in zip(loads, held, plan):
+        load.wait()
         for rows, columns, out, to_rows, to_columns in moves:
-            copies.append(
+            stores.append(
                 pltpu.make_async_copy(
-                    sources[piece].at[pl.ds(*rows), pl.ds(*columns)],
+                    buffer.at[pl.ds(*rows), pl.ds(*columns)],
                     outs[out].at[places_ref[place], pl.ds(*to_rows), pl.ds(*to_columns)],
-                    sems.at[len(copies)],
+                    stored.at[len(stores)],
                 )
             )
-            copies[-1].start()
-    for copy in copies:
-        copy.wait()
+            stores[-1].start()
+    for store in stores:
+        store.wait()
 
 
 def whole_call(kernel, rank, args, shapes, dtype):
@@ -193,17 +199,17 @@
 
 
 def assemble(plan, places, pieces, shapes):
-    count = sum(len(moves) for piece, place, moves in plan)
-    moved = 2 * sum(piece.size * piece.dtype.itemsize for piece in pieces)
+    count = sum(len(moves) for place, moves in plan)
     return pl.pallas_call(
         functools.partial(assemble_kernel, plan, len(pieces)),
         in_specs=[pl.BlockSpec(memory_space=pltpu.SMEM)]
-        + [pl.BlockSpec(memory_space=pltpu.VMEM)] * len(pieces),
+        + [pl.BlockSpec(memory_space=pl.ANY)] * len(pieces),
         out_specs=[pl.BlockSpec(memory_space=pl.ANY)] * len(shapes),
         out_shape=[jax.ShapeDtypeStruct(shape, BF16) for shape in shapes],
-        scratch_shapes=[pltpu.SemaphoreType.DMA((count,))],
-        compiler_params=pltpu.CompilerParams(vmem_limit_bytes=24 * 1024 * 1024),
-        cost_estimate=pl.CostEstimate(flops=0, bytes_accessed=moved, transcendentals=0),
+        scratch_shapes=[pltpu.VMEM(piece.shape, BF16) for piece in pieces]
+        + [pltpu.SemaphoreType.DMA((len(pieces),)), pltpu.SemaphoreType.DMA((count,))],
+        compiler_params=pltpu.CompilerParams(vmem_limit_bytes=40 * 1024 * 1024),
+        cost_estimate=pl.CostEstimate(flops=0, bytes_accessed=1 << 20, transcendentals=0),
     )(places, *pieces)
 
 
@@ -277,7 +283,6 @@
 
     me = g * 4 + core * 2 + x
     rank = jnp.reshape(core * 2 + x, (1,)).astype(jnp.int32)
-    lane = width // 2
     hidden_rows = mlp_out.shape[0]
     head_cut = (head_start, rank_heads, DH)
     hidden_cut = (functools.partial(hidden_start, hidden_rows), n_g, hidden_rows)
@@ -333,17 +338,16 @@
         return (own, from_x, pin(from_core))
 
     def in_order(state, *extra):
-        shapes = [(4 * own_rows, lane)] * 2
-        return whole_call(order_kernel, rank, list(exchange_end(state)) + list(extra), shapes, BF16)
+        values = list(exchange_end(state)) + list(extra)
+        return whole_call(order_kernel, rank, values, [(4 * own_rows, width)], BF16)[0]
 
     pieces = {}
-    lanes_left = {"self": 2, "cross": 2, "in": 2, "down": 2}
+    under_way = {"self", "cross", "in", "down"}
     sums = {}
     places = jnp.stack([g_at(offset) for offset in range(n_g)]).astype(jnp.int32)
 
-    def gather_task(name, side, block):
-        found = pieces.setdefault((name, side), [])
-        found.append((block, 0, 0))
+    def gather_task(name, block):
+        found = pieces.setdefault(name, [(block, 0, 0)])
         clock = counter = block
         half = block.shape[0] // 2
         for step in range(1, half_ring + 1):
@@ -352,16 +356,21 @@
             clock, counter = yield [(clock, go_next), (counter, go_prev)]
             found.append((clock, -step % n_g, 0))
             found.append((counter, step, half if step == half_ring else 0))
-        lanes_left[name] -= 1
-
-    def reduce_task(name, value, column):
-        rows_of = value.shape[1]
-
+        under_way.remove(name)
+
+    def reduce_task(name, *parts):
         def mine(offset):
-            return lax.dynamic_slice(value, (g_at(offset), 0, column), (1, rows_of, lane))[0]
+            where = g_at(offset)
+            blocks = []
+            for part in parts:
+                block = lax.dynamic_index_in_dim(part, where, 0, keepdims=False)
+                if block.shape[0] != parts[0].shape[1]:
+                    block = jnp.concatenate(jnp.split(block, 4, axis=1))
+                blocks.append(block)
+            return jnp.concatenate(blocks, axis=1) if len(blocks) > 1 else blocks[0]
 
         block = mine(half_ring)
-        half = rows_of // 2
+        half = block.shape[0] // 2
         clock, counter = block[:half], block[half:]
         for step in range(half_ring - 1, -1, -1):
             clock, counter = yield [(clock, go_next), (counter, go_prev)]
@@ -374,70 +383,66 @@
                 clock, counter = (up + clock).astype(BF16), (down + counter).astype(BF16)
         sums[name] = up + clock + counter
 
-    waiting = [[], []]
-    flying = [None, None]
-    turn = 0
-
-    def launch(side):
-        if waiting[side] and flying[side] is None:
-            task, rounds, sends = waiting[side].pop(0)
+    waiting = []
+    flying = []
+
+    def launch():
+        if waiting and not flying:
+            task, sends = waiting.pop(0)
             if sends is None:
                 sends = next(task)
             else:
                 values = pin(*[value for value, pairs in sends])
-                values = values if len(sends) > 1 else [values]
                 sends = [(value, pairs) for value, (old, pairs) in zip(values, sends)]
-            flying[side] = (task, rounds, [send(*item) for item in sends])
-
-    def enter(side, task, rounds=0):
-        waiting[side].append((task, rounds, None))
-        launch(side)
-
-    def visit(side):
-        if flying[side] is None:
-            return
-        task, rounds, flight = flying[side]
-        values = pin(*flight)
-        flying[side] = None
-        try:
-            sends = task.send(values)
-            if rounds == 1:
-                waiting[side].append((task, 0, sends))
-            else:
-                flying[side] = (task, rounds - 1, [send(*item) for item in sends])
-        except StopIteration:
-            pass
-        launch(side)
-
-    def ring(steps):
-        nonlocal turn
-        for unused in range(steps):
-            visit(turn)
-            turn ^= 1
+            flying.append((task, [send(*item) for item in sends]))
+
+    def enter(task):
+        waiting.append((task, None))
+        launch()
+
+    def ring(hold=False):
+        held = None
+        if flying:
+            task, flight = flying.pop()
+            try:
+                sends = task.send(pin(*flight))
+                if hold:
+                    held = (task, sends)
+                else:
+                    flying.append((task, [send(*item) for item in sends]))
+            except StopIteration:
+                pass
+            launch()
+        return held
+
+    def ring_with(*values):
+        task, flight = flying.pop()
+        got = pin(*flight, *values)
+        flying.append((task, list(got[: len(flight)])))
+        ring()
+        return got[len(flight) :]
 
     def settle(name, shapes, moves):
-        while lanes_left[name]:
-            ring(1)
+        while name in under_way:
+            ring()
         plan = []
-        values = []
-        for side in range(2):
-            for value, place, low in pieces[name, side]:
-                high = low + value.shape[0]
-                inside = []
-                for (row, size), columns, out, (to_row, unused), to_columns in moves[side]:
-                    first, last = max(row, low), min(row + size, high)
-                    if first < last:
-                        to = (to_row + first - row, last - first)
-                        inside.append(((first - low, last - first), columns, out, to, to_columns))
-                plan.append((len(values), place, inside))
-                values.append(value)
+        for value, place, low in pieces[name]:
+            high = low + value.shape[0]
+            inside = []
+            for (row, size), columns, out, (to_row, unused), to_columns in moves:
+                first, last = max(row, low), min(row + size, high)
+                if first < last:
+                    to = (to_row + first - row, last - first)
+                    inside.append(((first - low, last - first), columns, out, to, to_columns))
+            plan.append((place, inside))
+        values = [value for value, place, low in pieces[name]]
         shapes = [(n_g,) + shape for shape in shapes]
         outs = assemble(plan, places, values, shapes)
         return [out.reshape(n_g * out.shape[1], out.shape[2]) for out in outs]
 
     def summed(name):
         while name not in sums:
-            ring(1)
+            ring()
         return sums[name]
 
     def join_near(value, from_core):
@@ -463,12 +468,11 @@
     block_rows = 4 * own_rows
     block = (0, block_rows)
     stacked = [
-        ((part * own_rows, own_rows), (rank_width, rank_width), 1, (0, own_rows), (part * rank_width, rank_width))
+        ((part * own_rows, own_rows), (3 * rank_width, rank_width), 1, (0, own_rows), (part * rank_width, rank_width))
         for part in range(4)
     ]
 
-    for side in range(2):
-        enter(side, gather_task("down", side, mlp_out[:, side * lane : (side + 1) * lane]), 1)
+    enter(gather_task("down", mlp_out))
     qkv_state = exchange_x(cut_columns([attn_query, attn_key, attn_value], head_cut))
     vectors = jnp.stack(
         [
@@ -484,7 +488,6 @@
     ).astype(F32)[None]
 
     bits = n.bit_length() - 1
-    later = [None, None]
     out_block = send(attn_out, to_ranks)
     for bit in range(bits):
         other = pin(send(vectors, [(i, i ^ (1 << bit)) for i in range(n)]))
@@ -495,11 +498,8 @@
         if bit == 1:
             qkv_state = exchange_core(qkv_state)
         if bit == 2:
-            qkv_lanes = in_order(qkv_state, pin(out_block))
-            for side in range(2):
-                enter(side, gather_task("self", side, qkv_lanes[side]))
-                visit(side)
-                later[side] = waiting[side].pop(0)
+            enter(gather_task("self", in_order(qkv_state, pin(out_block))))
+            later = ring(hold=True)
     whole_vectors = vectors.transpose(1, 0, 2).reshape(8, width)
     embed, g_attn, b_attn, g_cross, b_cross, g_mlp, b_mlp = [whole_vectors[k] for k in range(7)]
 
@@ -511,14 +511,13 @@
     from_core = send(normed_one, swap_core)
     cross_blocks = pin(*cut_columns([cross_key, cross_value, cross_query], head_cut))
     one_near = join_near(normed_one, pin(from_core))
-    ring(2)
+    ring()
     from_x = pin(from_x)
     cross_state = exchange_x(cross_blocks)
+    cross_out_block = send(cross_out, to_ranks)
     one_far = jnp.concatenate([from_x, pin(send(from_x, swap_core))])
-    cross_out_block = send(cross_out, to_ranks)
-    ring(1)
     cross_state = exchange_core(cross_state)
-    ring(1)
+    ring()
     half_text = jnp.stack(
         [
             jnp.where(x == 1, text_states[1], text_states[0]),
@@ -528,15 +527,15 @@
     half_text, cross_out_block = pin(half_text, cross_out_block)
     text_x = send(half_text, swap_x)
     text_core = send(half_text, swap_core)
-    cross_lanes = in_order(cross_state, cross_out_block)
-    for side in range(2):
-        enter(side, gather_task("cross", side, cross_lanes[side]))
+    enter(gather_task("cross", in_order(cross_state, cross_out_block)))
     in_blocks = pin(*cut_columns([mlp_in], hidden_cut))
-    ring(1)
     text_x, text_core = pin(text_x, text_core)
     in_state = exchange_x(in_blocks)
     text_diagonal = pin(send(text_x, swap_core))
-    ring(1)
+    ring()
+    in_state = exchange_core(in_state)
+    back_x = send(out_grad, swap_x)
+    back_core = send(out_grad, swap_core)
     text_rows = pin(
         jnp.concatenate(
             [
@@ -551,15 +550,9 @@
             ]
         )
     )
-    in_state = exchange_core(in_state)
-    ring(1)
-    back_x = send(out_grad, swap_x)
-    back_core = send(out_grad, swap_core)
-    in_lanes = in_order(in_state)
-    for side in range(2):
-        enter(side, gather_task("in", side, in_lanes[side]))
-        waiting[side].append(later[side])
-    ring(1)
+    enter(gather_task("in", in_order(in_state)))
+    ring()
+    waiting.append(later)
 
     pair_rows = 2 * rows
     score_flops = 2 * 2 * images * rank_heads * L * DH
@@ -588,69 +581,64 @@
     w_qkv, w_out = settle(
         "self",
         [(block_rows, 3 * rank_width), (own_rows, width)],
-        [
-            [(block, (0, lane), 0, block, (0, lane))],
-            [(block, (0, rank_width), 0, block, (lane, rank_width))] + stacked,
-        ],
-    )
+        [(block, (0, 3 * rank_width), 0, block, (0, 3 * rank_width))] + stacked,
+    )
+    back_x, back_core = pin(back_x, back_core)
     qkv_far = pin(product(one_far, w_qkv).astype(BF16))
+    ring()
     mixed_far = self_forward(qkv_far)
     out_far = pin(product(mixed_far, w_out).astype(BF16))
     from_x = send_far(pair(out_far))
-    ring(2)
     qkv_near = pin(product(one_near, w_qkv).astype(BF16))
     mixed_near = self_forward(qkv_near)
     out_near = pair(pin(product(mixed_near, w_out)))
     from_core = pin(send(out_near[1].astype(BF16), swap_core))
-    back_x, back_core = pin(back_x, back_core)
+    ring()
     back_near = join_near(out_grad, back_core)
     back_far = jnp.concatenate([back_x, send(back_x, swap_core)])
-    ring(2)
     first = start + add_near(out_near[0], from_core, pin(from_x))
 
     unit_two, inverse_two = normalize(first)
     first, normed_two = pin(first, (unit_two * g_cross + b_cross).astype(BF16))
     from_x = send(normed_two, swap_x)
     two_near = join_near(normed_two, pin(send(normed_two, swap_core)))
-    ring(2)
+    ring()
     from_x = pin(from_x)
     two_far = jnp.concatenate([from_x, pin(send(from_x, swap_core))])
-    ring(2)
+    ring()
     w_text, w_cross_out, w_cross = settle(
         "cross",
-        [(block_rows, lane), (own_rows, width), (block_rows, rank_width)],
+        [(block_rows, 2 * rank_width), (own_rows, width), (block_rows, rank_width)],
         [
-            [(block, (0, lane), 0, block, (0, lane))],
-            [(block, (0, rank_width), 2, block, (0, rank_width))] + stacked,
-        ],
+            (block, (0, 2 * rank_width), 0, block, (0, 2 * rank_width)),
+            (block, (2 * rank_width, rank_width), 2, block, (0, rank_width)),
+        ]
+        + stacked,
     )
     text_kv = pin(product(text_rows, w_text).astype(BF16))
+    ring()
     cross_far = product(two_far, w_cross).astype(BF16)
     cmixed_far = cross_forward(cross_far, text_kv, 2 * images)
     out_far = pin(product(cmixed_far, w_cross_out).astype(BF16))
     from_x = send_far(pair(out_far))
-    ring(1)
     cross_near = product(two_near, w_cross).astype(BF16)
     cmixed_near = cross_forward(cross_near, text_kv, 0)
     out_near = pair(pin(product(cmixed_near, w_cross_out)))
     from_core = pin(send(out_near[1].astype(BF16), swap_core))
-    ring(1)
+    ring()
     second = first + add_near(out_near[0], from_core, pin(from_x))
 
     unit_three, inverse_three = normalize(second)
     second, normed_three = pin(second, (unit_three * g_mlp + b_mlp).astype(BF16))
     from_x = send(normed_three, swap_x)
     three_near = join_near(normed_three, pin(send(normed_three, swap_core)))
-    ring(2)
+    ring()
     from_x = pin(from_x)
     three_far = jnp.concatenate([from_x, pin(send(from_x, swap_core))])
     three_all = jnp.concatenate([three_near, three_far])
-    ring(2)
-    ring(2)
+    ring()
     (w_in,) = settle(
-        "in",
-        [(block_rows, width)],
-        [[(block, (0, lane), 0, block, (side * lane, lane))] for side in range(2)],
+        "in", [(block_rows, width)], [(block, (0, width), 0, block, (0, width))]
     )
 
     def feed(values):
@@ -660,33 +648,35 @@
         return pin((hidden_pre * share).astype(BF16), share + hidden_pre * bell)
 
     activated_near, slope_near = feed(three_near)
-    ring(1)
+    ring()
     activated_far, slope_far = feed(three_far)
-    ring(1)
+    ring()
     activated = jnp.concatenate([activated_near, activated_far])
     back_all = jnp.concatenate([back_near, back_far])
     down_part = pin(outer_grad(activated, back_all).astype(BF16)).reshape(n_g, hidden_rows, width)
-    ring(2)
-    for side in range(2):
-        enter(side, reduce_task(("down", side), down_part, side * lane))
-    ring(2)
+    enter(reduce_task("down", down_part))
+    ring()
 
     down_block = (0, hidden_rows)
     (w_down,) = settle(
-        "down",
-        [(hidden_rows, width)],
-        [[(down_block, (0, lane), 0, down_block, (side * lane, lane))] for side in range(2)],
-    )
+        "down", [(hidden_rows, width)], [(down_block, (0, width), 0, down_block, (0, width))]
+    )
+    w_down = pin(w_down)
+    ring()
     hidden_far = pin((back_project(back_far, w_down) * slope_far).astype(BF16))
-    ring(1)
+    ring()
     three_grad = pin(back_project(hidden_far, w_in).astype(BF16))
     from_x = send_far(pair(three_grad))
-    ring(1)
     hidden_near = pin((back_project(back_near, w_down) * slope_near).astype(BF16))
+    (from_x,) = ring_with(from_x)
+    hidden_all = jnp.concatenate([hidden_near, hidden_far])
+    in_part = pin(outer_grad(three_all, hidden_all).astype(BF16))
+    in_part = in_part.reshape(n_g, block_rows, hidden // 4)
+    enter(reduce_task("in", in_part))
+    ring()
     three_grad = pair(pin(back_project(hidden_near, w_in)))
     from_core = pin(send(three_grad[1].astype(BF16), swap_core))
-    ring(2)
-    normed_three_grad = add_near(three_grad[0], from_core, pin(from_x))
+    normed_three_grad = add_near(three_grad[0], from_core, from_x)
     rows_three, gain_mlp_term, bias_mlp_term = norm_backward(
         normed_three_grad, unit_three, inverse_three, g_mlp
     )
@@ -696,12 +686,7 @@
     )
     from_x = send(second_low, swap_x)
     second_near = join_near(second_low, pin(send(second_low, swap_core)))
-    hidden_all = jnp.concatenate([hidden_near, hidden_far])
-    in_part = pin(outer_grad(three_all, hidden_all).astype(BF16))
-    in_part = in_part.reshape(n_g, block_rows, hidden // 4)
-    for side in range(2):
-        enter(side, reduce_task(("in", side), in_part, side * lane))
-    ring(2)
+    ring()
 
     def by_target(total):
         def rows_of(rel):
@@ -709,11 +694,6 @@
             return lax.dynamic_slice(total, (low, 0), (own_rows, total.shape[1])).astype(BF16)
 
         return (rows_of(0), jnp.stack([rows_of(1), rows_of(3)]), rows_of(2))
-
-    def stack_rows(part):
-        cut = part.reshape(n_g, own_rows, width)
-        size = width // 4
-        return jnp.concatenate([cut[:, :, k * size : (k + 1) * size] for k in range(4)], axis=1)
 
     def unstack_rows(total):
         return jnp.concatenate(
@@ -737,37 +717,43 @@
     cq_far, tkv_far = cross_backward(cross_far, text_kv, cgrad_far, 2 * images)
     two_grad = pin(back_project(cq_far, w_cross).astype(BF16))
     from_x = send_far(pair(two_grad))
-    ring(2)
+    second_near = pin(second_near)
     cgrad_near = back_project(second_near, w_cross_out).astype(BF16)
     cq_near, tkv_near = cross_backward(cross_near, text_kv, cgrad_near, 0)
     two_grad = pair(pin(back_project(cq_near, w_cross)))
     from_core = pin(send(two_grad[1].astype(BF16), swap_core))
+    (from_x,) = ring_with(from_x)
+    cq_near, cq_far, tkv_near, tkv_far, second_far = pin(
+        cq_near, cq_far, tkv_near, tkv_far, second_far
+    )
+    normed_two_grad = add_near(two_grad[0], from_core, from_x)
+    rows_two, gain_cross_term, bias_cross_term = norm_backward(
+        normed_two_grad, unit_two, inverse_two, g_cross
+    )
+    first_grad = second_grad + rows_two
+    first_grad, gain_cross_term, bias_cross_term, first_low = pin(
+        first_grad, gain_cross_term, bias_cross_term, first_grad.astype(BF16)
+    )
+    from_x = send(first_low, swap_x)
+    first_near = join_near(first_low, pin(send(first_low, swap_core)))
     cmixed_all = jnp.concatenate([cmixed_near, cmixed_far])
     second_all = jnp.concatenate([second_near, second_far])
     cross_out_part = pin(outer_grad(cmixed_all, second_all).astype(BF16))
-    ring(2)
-    normed_two_grad = add_near(two_grad[0], from_core, pin(from_x))
-    rows_two, gain_cross_term, bias_cross_term = norm_backward(
-        normed_two_grad, unit_two, inverse_two, g_cross
-    )
-    first_grad = second_grad + rows_two
-    first_grad, gain_cross_term, bias_cross_term, first_low = pin(
-        first_grad, gain_cross_term, bias_cross_term, first_grad.astype(BF16)
-    )
-    from_x = send(first_low, swap_x)
-    first_near = join_near(first_low, pin(send(first_low, swap_core)))
     two_all = jnp.concatenate([two_near, two_far])
     cq_all = jnp.concatenate([cq_near, cq_far])
     tkv_all = jnp.concatenate([tkv_near, tkv_far])
     cross_part = pin(outer_grad(two_all, cq_all).astype(BF16))
-    ring(1)
+    (from_x,) = ring_with(from_x)
+    tkv_all, first_near = pin(tkv_all, first_near)
     text_kv_part = pin(outer_grad(text_rows, tkv_all).astype(BF16))
-    text_kv_part = text_kv_part.reshape(n_g, block_rows, lane)
-    cross_part = cross_part.reshape(n_g, block_rows, rank_width)
-    cross_part = jnp.concatenate([cross_part, stack_rows(cross_out_part)], axis=2)
-    enter(0, reduce_task(("cross", 0), text_kv_part, 0))
-    enter(1, reduce_task(("cross", 1), cross_part, 0))
-    ring(1)
+    enter(
+        reduce_task(
+            "cross",
+            text_kv_part.reshape(n_g, block_rows, 2 * rank_width),
+            cross_part.reshape(n_g, block_rows, rank_width),
+            cross_out_part.reshape(n_g, own_rows, width),
+        )
+    )
     sgrad_near = pin(back_project(first_near, w_out).astype(BF16))
 
     def self_backward(qkv, grads):
@@ -781,30 +767,32 @@
         )[0]
 
     qkv_grad_near = pin(self_backward(qkv_near, sgrad_near))
+    ring()
     from_x = pin(from_x)
     first_far = jnp.concatenate([from_x, pin(send(from_x, swap_core))])
-    ring(2)
     sgrad_far = back_project(first_far, w_out).astype(BF16)
-    qkv_grad_far = self_backward(qkv_far, sgrad_far)
+    qkv_grad_far = pin(self_backward(qkv_far, sgrad_far))
+    ring()
     one_grad = pin(back_project(qkv_grad_far, w_qkv).astype(BF16))
     from_x = send_far(pair(one_grad))
-    ring(1)
     one_all = jnp.concatenate([one_near, one_far])
     qkv_grad_all = jnp.concatenate([qkv_grad_near, qkv_grad_far])
     qkv_part = pin(outer_grad(one_all, qkv_grad_all).astype(BF16))
-    ring(1)
+    (from_x,) = ring_with(from_x)
+    first_far, qkv_grad_near = pin(first_far, qkv_grad_near)
     mixed_all = jnp.concatenate([mixed_near, mixed_far])
     first_all = jnp.concatenate([first_near, first_far])
     out_part = pin(outer_grad(mixed_all, first_all).astype(BF16))
-    qkv_part = qkv_part.reshape(n_g, block_rows, 3 * rank_width)
-    enter(0, reduce_task(("self", 0), qkv_part, 0))
-    last_part = jnp.concatenate([qkv_part[:, :, lane:], stack_rows(out_part)], axis=2)
-    enter(1, reduce_task(("self", 1), last_part, 0))
-    ring(1)
+    enter(
+        reduce_task(
+            "self",
+            qkv_part.reshape(n_g, block_rows, 3 * rank_width),
+            out_part.reshape(n_g, own_rows, width),
+        )
+    )
     one_grad = pair(pin(back_project(qkv_grad_near, w_qkv)))
     from_core = pin(send(one_grad[1].astype(BF16), swap_core))
-    ring(1)
-    normed_one_grad = add_near(one_grad[0], from_core, pin(from_x))
+    normed_one_grad = add_near(one_grad[0], from_core, from_x)
     rows_one, gain_attn_term, bias_attn_term = norm_backward(
         normed_one_grad, unit_one, inverse_one, g_attn
     )
@@ -814,23 +802,29 @@
     tokens_grad, embed_term, gain_attn_term, bias_attn_term = pin(
         tokens_grad, embed_term, gain_attn_term, bias_attn_term
     )
-
+    ring()
+
+    activated_far, activated_near, tkv_all = pin(activated_far, activated_near, tkv_all)
     result_far = pin(product(activated_far, w_down).astype(BF16))
-    ring(1)
     from_x = send_far(pair(result_far))
     result_near = pair(pin(product(activated_near, w_down)))
     from_core = pin(send(result_near[1].astype(BF16), swap_core))
-    ring(2)
+    (from_x,) = ring_with(from_x)
+    tkv_all = pin(tkv_all)
     text_part = pin(back_project(tkv_all, w_text)).reshape(8, ctx // 2, width)
-    output = pin((second + add_near(result_near[0], from_core, pin(from_x))).astype(BF16))
+    output = pin((second + add_near(result_near[0], from_core, from_x)).astype(BF16))
+    ring()
     text_own = jnp.stack([text_part[0], text_part[4]])
     text_far = [
         jnp.stack([text_part[a], text_part[b]]).astype(BF16) for a, b in ((5, 1), (2, 6), (7, 3))
     ]
     from_x = send_far([text_far[0], text_far[2]])
     from_core = pin(send(text_far[1], swap_core))
-    ring(2)
+    in_sum, mlp_out_grad = pin(summed("in"), summed("down"))
+    in_state = exchange_x(by_target(in_sum))
     text_sum = add_near(text_own, from_core, pin(from_x))
+    in_state = exchange_core(in_state)
+    ring()
     text_grad = pin(
         jnp.stack(
             [
@@ -839,13 +833,19 @@
             ]
         )
     )
-    in_sum = jnp.concatenate([summed(("in", 0)), summed(("in", 1))], axis=1)
-    in_state = exchange_core(exchange_x(by_target(in_sum)))
-    ring(2)
     (mlp_in_grad,) = join_columns(*exchange_end(in_state), hidden_cut, 1)
     mlp_in_grad = pin(mlp_in_grad)
-    mlp_out_grad = pin(jnp.concatenate([summed(("down", 0)), summed(("down", 1))], axis=1))
-
+
+    cross_sum = summed("cross")
+    cross_state = exchange_x(by_target(cross_sum[:, : 3 * rank_width]))
+    cross_out_grad = send(unstack_rows(cross_sum[:, 3 * rank_width :]), from_ranks)
+    cross_state = exchange_core(cross_state)
+    cross_key_grad, cross_value_grad, cross_query_grad = join_columns(
+        *exchange_end(cross_state), head_cut, 3
+    )
+    cross_query_grad, cross_key_grad, cross_value_grad, cross_out_grad = pin(
+        cross_query_grad, cross_key_grad, cross_value_grad, cross_out_grad.astype(F32)
+    )
     terms = jnp.stack(
         [
             embed_term,
@@ -867,25 +867,9 @@
         terms = keep + pin(send(away, [(i, i ^ (1 << bit)) for i in range(n)]))
     terms = terms[0]
 
-    text_kv_sum = summed(("cross", 0))
-    cross_sum = summed(("cross", 1))
-    cross_total = jnp.concatenate([text_kv_sum, cross_sum[:, :rank_width]], axis=1)
-    cross_state = exchange_x(by_target(cross_total))
-    cross_out_grad = send(unstack_rows(cross_sum[:, rank_width:]), from_ranks)
-    ring(1)
-    cross_state = exchange_core(cross_state)
-    ring(1)
-    cross_key_grad, cross_value_grad, cross_query_grad = join_columns(
-        *exchange_end(cross_state), head_cut, 3
-    )
-    cross_query_grad, cross_key_grad, cross_value_grad, cross_out_grad = pin(
-        cross_query_grad, cross_key_grad, cross_value_grad, cross_out_grad.astype(F32)
-    )
-    qkv_sum = summed(("self", 0))
-    last_sum = summed(("self", 1))
-    qkv_sum = jnp.concatenate([qkv_sum, last_sum[:, :rank_width]], axis=1)
-    attn_out_grad = send(unstack_rows(last_sum[:, rank_width:]), from_ranks).astype(F32)
-    qkv_state = exchange_core(exchange_x(by_target(qkv_sum)))
+    self_sum = summed("self")
+    attn_out_grad = send(unstack_rows(self_sum[:, 3 * rank_width :]), from_ranks).astype(F32)
+    qkv_state = exchange_core(exchange_x(by_target(self_sum[:, : 3 * rank_width])))
     attn_query_grad, attn_key_grad, attn_value_grad = join_columns(
         *exchange_end(qkv_state), head_cut, 3
     )

time: 1040 us -> 997 us (0.959)
  starting transfers between devices: 221 us -> 156 us
  waiting for transfers between devices: 448 us -> 476 us
    ppermute x196 -> x132, starting transfers between devices: 221 us -> 156 us  [send(): return lax.ppermute(value, AXES, pairs)]
    ppermute x196 -> x132, waiting for transfers between devices: 448 us -> 476 us  [send(): return lax.ppermute(value, AXES, pairs)]
    unnamed x492 -> x383, local copies, waits for them, and re-layouts: 37.8 us -> 25.8 us
    pallas_call x4, Pallas kernels: 10.3 us -> 21 us  [assemble(): pl.pallas_call(functools.partial(assemble_kernel, plan, len(pieces)), in_...]
  transfers between devices with their start and end apart: 196 -> 132, of which waited for: 87 -> 68; matrix products, arithmetic and copies ran while one was open for 22% -> 22% of each run, Pallas kernels for 3% -> 4%
where the time goes in v2:
time: 997 us; the launch traced here: 987 us
  waiting for transfers between devices  476 us (48%)
  starting transfers between devices  156 us (16%)
  matrix products  154 us (15%)
  other arithmetic  86.2 us (9%)
  local copies, waits for them, and re-layouts  59.9 us (6%)
  Pallas kernels  50.1 us (5%)
    ppermute x132, waiting for transfers between devices, send(): return lax.ppermute(value, AXES, pairs)  476 us
    ppermute x132, starting transfers between devices, send(): return lax.ppermute(value, AXES, pairs)  156 us
    dot_general x13, matrix products, product(): return jnp.dot(left, right, preferred_element_type=F32)  54.4 us
    dot_general x13, matrix products, back_project(): lax.dot_general(left, right, (((1,), (1,)), ((), ())), preferred_element_...  53.4 us
    dot_general x7, matrix products, outer_grad(): lax.dot_general(left, right, (((0,), (0,)), ((), ())), preferred_element_...  46.6 us
    unnamed x383, local copies, waits for them, and re-layouts  25.8 us
    pallas_call x8, Pallas kernels, by_image(): pl.pallas_call(kernel, grid=(images,), in_specs=[pl.BlockSpec(block, func...  23.2 us
    pallas_call x4, Pallas kernels, assemble(): pl.pallas_call(functools.partial(assemble_kernel, plan, len(pieces)), in_...  21 us
  transfers between devices with their start and end apart: 132, of which 68 were waited for; matrix products, arithmetic and copies ran while one was open for 22% of the time, Pallas kernels for 4%

profile of v2, /device:TPU:3, one launch (start us, length us, event | category | flops | bytes accessed | tf_op | source)
XLA Modules:
  0.0 987.0 jit_solution(6234555439207307857)
XLA Ops:
  54.0 19.6 %collective-permute-done.11.refs_1_ = bf16[256,2048]{1,0:T(8,128)(2,1)S(1)} collective-permute-done((bf16[256,2048]{1,0:T(8,128)(2,1)S(1)}, bf16[256,2048]{1,0:T(8,128)(2,1)S(1)}, u32[]{:S(2)}, u32[]{:S(2)}) %collective-permute-start.11) | collective-permute-done | bytes 1048608 | tf_op jit(solution)/shard_map/ppermute | solution.py:271
  112.2 17.2 %collective-permute-done.21 = bf16[2,64,2048]{2,1,0:T(8,128)(2,1)S(1)} collective-permute-done((bf16[2,64,2048]{2,1,0:T(8,128)(2,1)S(1)}, bf16[2,64,2048]{2,1,0:T(8,128)(2,1)S(1)}, u32[]{:S(2)}, u32[]{:S(2)}) %collective-permute-start.21) | collective-permute-done | bytes 524320 | tf_op jit(solution)/shard_map/ppermute | solution.py:271
  136.8 16.1 %collective-permute-done.19.refs_6_ = bf16[256,2048]{1,0:T(8,128)(2,1)S(1)} collective-permute-done((bf16[256,2048]{1,0:T(8,128)(2,1)}, bf16[256,2048]{1,0:T(8,128)(2,1)S(1)}, u32[]{:S(2)}, u32[]{:S(2)}) %collective-permute-start.19) | collective-permute-done | bytes 1048608 | tf_op jit(solution)/shard_map/ppermute | solution.py:271
  209.7 20.1 %collective-permute-done.35.refs_3_ = bf16[256,2048]{1,0:T(8,128)(2,1)S(1)} collective-permute-done((bf16[256,2048]{1,0:T(8,128)(2,1)}, bf16[256,2048]{1,0:T(8,128)(2,1)S(1)}, u32[]{:S(2)}, u32[]{:S(2)}) %collective-permute-start.35) | collective-permute-done | bytes 1048608 | tf_op jit(solution)/shard_map/ppermute | solution.py:271
  241.5 22.0 %collective-permute-done.39.refs_5_ = bf16[256,2048]{1,0:T(8,128)(2,1)S(1)} collective-permute-done((bf16[256,2048]{1,0:T(8,128)(2,1)S(1)}, bf16[256,2048]{1,0:T(8,128)(2,1)S(1)}, u32[]{:S(2)}, u32[]{:S(2)}) %collective-permute-start.39) | collective-permute-done | bytes 1048608 | tf_op jit(solution)/shard_map/ppermute | solution.py:271
  269.4 10.1 %collective-permute-done.41.refs_7_ = bf16[128,2048]{1,0:T(8,128)(2,1)S(1)} collective-permute-done((bf16[128,2048]{1,0:T(8,128)(2,1)S(1)}, bf16[128,2048]{1,0:T(8,128)(2,1)S(1)}, u32[]{:S(2)}, u32[]{:S(2)}) %collective-permute-start.41) | collective-permute-done | bytes 524320 | tf_op jit(solution)/shard_map/ppermute | solution.py:271
  291.6 10.5 %collective-permute-done.45.refs_1_ = bf16[256,2048]{1,0:T(8,128)(2,1)} collective-permute-done((bf16[256,2048]{1,0:T(8,128)(2,1)S(1)}, bf16[256,2048]{1,0:T(8,128)(2,1)}, u32[]{:S(2)}, u32[]{:S(2)}) %collective-permute-start.45) | collective-permute-done | bytes 1048608 | tf_op jit(solution)/shard_map/ppermute | solution.py:271
  319.2 21.6 %collective-permute-done.49.refs_3_ = bf16[256,2048]{1,0:T(8,128)(2,1)S(1)} collective-permute-done((bf16[256,2048]{1,0:T(8,128)(2,1)}, bf16[256,2048]{1,0:T(8,128)(2,1)S(1)}, u32[]{:S(2)}, u32[]{:S(2)}) %collective-permute-start.49) | collective-permute-done | bytes 1048608 | tf_op jit(solution)/shard_map/ppermute | solution.py:271
  350.9 21.6 %collective-permute-done.53.refs_5_ = bf16[256,2048]{1,0:T(8,128)(2,1)S(1)} collective-permute-done((bf16[256,2048]{1,0:T(8,128)(2,1)S(1)}, bf16[256,2048]{1,0:T(8,128)(2,1)S(1)}, u32[]{:S(2)}, u32[]{:S(2)}) %collective-permute-start.53) | collective-permute-done | bytes 1048608 | tf_op jit(solution)/shard_map/ppermute | solution.py:271
  379.3 10.9 %collective-permute-done.57.refs_7_ = bf16[128,2048]{1,0:T(8,128)(2,1)} collective-permute-done((bf16[128,2048]{1,0:T(8,128)(2,1)}, bf16[128,2048]{1,0:T(8,128)(2,1)}, u32[]{:S(2)}, u32[]{:S(2)}) %collective-permute-start.57) | collective-permute-done | bytes 524320 | tf_op jit(solution)/shard_map/ppermute | solution.py:271
  401.7 10.1 %fusion.7 = (f32[512,2048]{1,0:T(8,128)}, bf16[512,2048]{1,0:T(8,128)(2,1)}) fusion(bf16[2048,2048]{1,0:T(8,128)(2,1)} %bitcast.315, bf16[256,2048]{1,0:T(8,128)(2,1)S(1)} %copy-done.172, bf16[256,2048]{1,0:T(8,128)(2,1)S(1)} %copy-done.100), kind=kOutput, calls=%fused_computation.12 | convolution fusion | flops 4309647360 | bytes 16777216 | tf_op jit(solution)/shard_map/dot_general | solution.py:34
  422.8 11.8 %convolution_convert_fusion.2 = bf16[2048,2048]{1,0:T(8,128)(2,1)S(1)} fusion(bf16[512,2048]{1,0:T(8,128)(2,1)} %get-tuple-element.722, bf16[512,2048]{1,0:T(8,128)(2,1)} %get-tuple-element.721, bf16[256,2048]{1,0:T(8,128)(2,1)} %collective-permute-done.65, bf16[256,2048]{1,0:T(8,128)(2,1)S(1)} %copy-done.169, ...), kind=kOutput, calls=%fused_computation.2 | convolution fusion | flops 8619294720 | bytes 16777216 | tf_op jit(solution)/shard_map/dot_general | solution.py:38
  434.7 9.5 collective-permute-done.61.refs_5_
  469.9 9.7 multiply_convert_fusion
  522.6 14.3 %convolution_convert_fusion.1 = bf16[2048,2048]{1,0:T(8,128)(2,1)} fusion(bf16[256,2048]{1,0:T(8,128)(2,1)} %collective-permute-done.56, bf16[256,2048]{1,0:T(8,128)(2,1)} %collective-permute-done.52, bf16[256,2048]{1,0:T(8,128)(2,1)} %copy-done.171, bf16[256,2048]{1,0:T(8,128)(2,1)} %copy-done.99, bf16[512,2048]{1,0:T(8,128)(2,1)} %multiply_convert_fusion, ...), kind=kOutput, calls=%fused_computation.1 | convolution fusion | flops 8619294720 | bytes 16777216 | tf_op jit(solution)/shard_map/dot_general | solution.py:38
  555.9 16.9 %collective-permute-done.74 = bf16[256,2048]{1,0:T(8,128)(2,1)S(1)} collective-permute-done((bf16[256,2048]{1,0:T(8,128)(2,1)S(1)}, bf16[256,2048]{1,0:T(8,128)(2,1)S(1)}, u32[]{:S(2)}, u32[]{:S(2)}) %collective-permute-start.74) | collective-permute-done | bytes 1048608 | tf_op jit(solution)/shard_map/ppermute | solution.py:271
  585.7 11.6 %collective-permute-done.79 = bf16[128,2048]{1,0:T(8,128)(2,1)S(1)} collective-permute-done((bf16[128,2048]{1,0:T(8,128)(2,1)S(1)}, bf16[128,2048]{1,0:T(8,128)(2,1)S(1)}, u32[]{:S(2)}, u32[]{:S(2)}) %collective-permute-start.79) | collective-permute-done | bytes 524320 | tf_op jit(solution)/shard_map/ppermute | solution.py:271
  645.7 11.2 %collective-permute-done.84 = bf16[256,2048]{1,0:T(8,128)(2,1)} collective-permute-done((bf16[256,2048]{1,0:T(8,128)(2,1)}, bf16[256,2048]{1,0:T(8,128)(2,1)}, u32[]{:S(2)}, u32[]{:S(2)}) %collective-permute-start.84) | collective-permute-done | bytes 1048608 | tf_op jit(solution)/shard_map/ppermute | solution.py:271
  684.0 11.0 %collective-permute-done.88 = bf16[256,2048]{1,0:T(8,128)(2,1)} collective-permute-done((bf16[256,2048]{1,0:T(8,128)(2,1)}, bf16[256,2048]{1,0:T(8,128)(2,1)}, u32[]{:S(2)}, u32[]{:S(2)}) %collective-permute-start.88) | collective-permute-done | bytes 1048608 | tf_op jit(solution)/shard_map/ppermute | solution.py:271
  715.7 21.1 %collective-permute-done.93 = bf16[256,2048]{1,0:T(8,128)(2,1)S(1)} collective-permute-done((bf16[256,2048]{1,0:T(8,128)(2,1)S(1)}, bf16[256,2048]{1,0:T(8,128)(2,1)S(1)}, u32[]{:S(2)}, u32[]{:S(2)}) %collective-permute-start.93) | collective-permute-done | bytes 1048608 | tf_op jit(solution)/shard_map/ppermute | solution.py:271
  744.1 11.0 %collective-permute-done.115.from_x = bf16[2,64,2048]{2,1,0:T(8,128)(2,1)S(1)} collective-permute-done((bf16[2,64,2048]{2,1,0:T(8,128)(2,1)S(1)}, bf16[2,64,2048]{2,1,0:T(8,128)(2,1)S(1)}, u32[]{:S(2)}, u32[]{:S(2)}) %collective-permute-start.115) | collective-permute-done | bytes 524320 | tf_op jit(solution)/shard_map/ppermute | solution.py:271
  817.1 15.1 %collective-permute-done.109 = bf16[128,2048]{1,0:T(8,128)(2,1)S(1)} collective-permute-done((bf16[128,2048]{1,0:T(8,128)(2,1)S(1)}, bf16[128,2048]{1,0:T(8,128)(2,1)S(1)}, u32[]{:S(2)}, u32[]{:S(2)}) %collective-permute-start.109) | collective-permute-done | bytes 524320 | tf_op jit(solution)/shard_map/ppermute | solution.py:271
  906.1 30.3 %collective-permute-done.121 = bf16[256,2048]{1,0:T(8,128)(2,1)S(1)} collective-permute-done((bf16[256,2048]{1,0:T(8,128)(2,1)S(1)}, bf16[256,2048]{1,0:T(8,128)(2,1)S(1)}, u32[]{:S(2)}, u32[]{:S(2)}) %collective-permute-start.121) | collective-permute-done | bytes 1048608 | tf_op jit(solution)/shard_map/ppermute | solution.py:271
  953.1 13.6 %collective-permute-done.123 = bf16[256,2048]{1,0:T(8,128)(2,1)S(1)} collective-permute-done((bf16[256,2048]{1,0:T(8,128)(2,1)S(1)}, bf16[256,2048]{1,0:T(8,128)(2,1)S(1)}, u32[]{:S(2)}, u32[]{:S(2)}) %collective-permute-start.123) | collective-permute-done | bytes 1048608 | tf_op jit(solution)/shard_map/ppermute | solution.py:271
  (886 shorter events, 615.9 us)
Async XLA Ops:
  1.5 30.4 %collective-permute-start.5 = (bf16[256,2048]{1,0:T(8,128)(2,1)}, bf16[256,2048]{1,0:T(8,128)(2,1)S(1)}, u32[]{:S(2)}, u32[]{:S(2)}) collective-permute-start(bf16[256,2048]{1,0:T(8,128)(2,1)} %refs_0_.7), channel_id=1, source_target_pairs={{0,8},{1,9},{2,10},{3,11},{4,0},{5,1},{6,2},{7,3},{8,16},{9,17},{1... | collective-permute-start | bytes 3145736 | tf_op jit(solution)/shard_map/ppermute | solution.py:271
  76.1 30.5 %collective-permute-start.13 = (bf16[256,2048]{1,0:T(8,128)(2,1)S(1)}, bf16[256,2048]{1,0:T(8,128)(2,1)}, u32[]{:S(2)}, u32[]{:S(2)}) collective-permute-start(bf16[256,2048]{1,0:T(8,128)(2,1)S(1)} %collective-permute-done.11.refs_1_), channel_id=1, source_target_pairs={{0,8},{1,9},{2,10},{3,11},{4,0},{5,1},{6,2},{7,3},{8,16},{9,17},{1... | collective-permute-start | bytes 3145736 | tf_op jit(solution)/shard_map/ppermute | solution.py:271
  85.6 84.2 %collective-permute-start.29 = (bf16[256,2048]{1,0:T(8,128)(2,1)}, bf16[256,2048]{1,0:T(8,128)(2,1)S(1)}, u32[]{:S(2)}, u32[]{:S(2)}) collective-permute-start(bf16[256,2048]{1,0:T(8,128)(2,1)} %param.41), channel_id=1, source_target_pairs={{0,1},{1,0},{2,3},{3,2},{4,5},{5,4},{6,7},{7,6},{8,9},{9,8},{10,11... | collective-permute-start | bytes 3145736 | tf_op jit(solution)/shard_map/ppermute | solution.py:271
  95.8 75.0 %collective-permute-start.30 = (bf16[256,2048]{1,0:T(8,128)(2,1)}, bf16[256,2048]{1,0:T(8,128)(2,1)}, u32[]{:S(2)}, u32[]{:S(2)}) collective-permute-start(bf16[256,2048]{1,0:T(8,128)(2,1)} %param.41), channel_id=1, source_target_pairs={{0,2},{1,3},{2,0},{3,1},{4,6},{5,7},{6,4},{7,5},{8,10},{9,11},{10,... | collective-permute-start | bytes 3145736 | tf_op jit(solution)/shard_map/ppermute | solution.py:271
  267.7 34.4 %collective-permute-start.45 = (bf16[256,2048]{1,0:T(8,128)(2,1)S(1)}, bf16[256,2048]{1,0:T(8,128)(2,1)}, u32[]{:S(2)}, u32[]{:S(2)}) collective-permute-start(bf16[256,2048]{1,0:T(8,128)(2,1)S(1)} %shard_map.367.refs_0_), channel_id=1, source_target_pairs={{0,8},{1,9},{2,10},{3,11},{4,0},{5,1},{6,2},{7,3},{8,16},{9,17},{1... | collective-permute-start | bytes 3145736 | tf_op jit(solution)/shard_map/ppermute | solution.py:271
  269.2 34.2 %collective-permute-start.46 = (bf16[256,2048]{1,0:T(8,128)(2,1)S(1)}, bf16[256,2048]{1,0:T(8,128)(2,1)}, u32[]{:S(2)}, u32[]{:S(2)}) collective-permute-start(bf16[256,2048]{1,0:T(8,128)(2,1)S(1)} %shard_map.367.refs_0_), channel_id=1, source_target_pairs={{8,0},{9,1},{10,2},{11,3},{0,4},{1,5},{2,6},{3,7},{16,8},{17,9},{1... | collective-permute-start | bytes 3145736 | tf_op jit(solution)/shard_map/ppermute | solution.py:271
  378.7 44.1 %collective-permute-start.65 = (bf16[256,2048]{1,0:T(8,128)(2,1)}, bf16[256,2048]{1,0:T(8,128)(2,1)}, u32[]{:S(2)}, u32[]{:S(2)}) collective-permute-start(bf16[256,2048]{1,0:T(8,128)(2,1)} %copy-done.168), channel_id=1, source_target_pairs={{0,2},{1,3},{2,0},{3,1},{4,6},{5,7},{6,4},{7,5},{8,10},{9,11},{10,... | collective-permute-start | bytes 3145736 | tf_op jit(solution)/shard_map/ppermute | solution.py:271
  665.4 30.8 %collective-permute-start.90 = (bf16[256,2048]{1,0:T(8,128)(2,1)}, bf16[256,2048]{1,0:T(8,128)(2,1)}, u32[]{:S(2)}, u32[]{:S(2)}) collective-permute-start(bf16[256,2048]{1,0:T(8,128)(2,1)} %get-tuple-element.657), channel_id=1, source_target_pairs={{0,1},{1,0},{2,3},{3,2},{4,5},{5,4},{6,7},{7,6},{8,9},{9,8},{10,11... | collective-permute-start | bytes 3145736 | tf_op jit(solution)/shard_map/ppermute | solution.py:271
  702.4 60.3 %collective-permute-start.91 = (bf16[128,2048]{1,0:T(8,128)(2,1)S(1)}, bf16[128,2048]{1,0:T(8,128)(2,1)S(1)}, u32[]{:S(2)}, u32[]{:S(2)}) collective-permute-start(bf16[128,2048]{1,0:T(8,128)(2,1)S(1)} %get-tuple-element.919), channel_id=1, source_target_pairs={{0,8},{1,9},{2,10},{3,11},{4,0},{5,1},{6,2},{7,3},{8,16},{9,17},{1... | collective-permute-start | bytes 1572872 | tf_op jit(solution)/shard_map/ppermute | solution.py:271
  702.8 59.8 %collective-permute-start.92 = (bf16[128,2048]{1,0:T(8,128)(2,1)S(1)}, bf16[128,2048]{1,0:T(8,128)(2,1)S(1)}, u32[]{:S(2)}, u32[]{:S(2)}) collective-permute-start(bf16[128,2048]{1,0:T(8,128)(2,1)S(1)} %get-tuple-element.918), channel_id=1, source_target_pairs={{8,0},{9,1},{10,2},{11,3},{0,4},{1,5},{2,6},{3,7},{16,8},{17,9},{1... | collective-permute-start | bytes 1572872 | tf_op jit(solution)/shard_map/ppermute | solution.py:271
  706.8 30.0 %collective-permute-start.93 = (bf16[256,2048]{1,0:T(8,128)(2,1)S(1)}, bf16[256,2048]{1,0:T(8,128)(2,1)S(1)}, u32[]{:S(2)}, u32[]{:S(2)}) collective-permute-start(bf16[256,2048]{1,0:T(8,128)(2,1)S(1)} %get-tuple-element.831), channel_id=1, source_target_pairs={{0,8},{1,9},{2,10},{3,11},{4,0},{5,1},{6,2},{7,3},{8,16},{9,17},{1... | collective-permute-start | bytes 3145736 | tf_op jit(solution)/shard_map/ppermute | solution.py:271
  707.4 29.5 %collective-permute-start.94 = (bf16[256,2048]{1,0:T(8,128)(2,1)S(1)}, bf16[256,2048]{1,0:T(8,128)(2,1)S(1)}, u32[]{:S(2)}, u32[]{:S(2)}) collective-permute-start(bf16[256,2048]{1,0:T(8,128)(2,1)S(1)} %get-tuple-element.830), channel_id=1, source_target_pairs={{8,0},{9,1},{10,2},{11,3},{0,4},{1,5},{2,6},{3,7},{16,8},{17,9},{1... | collective-permute-start | bytes 3145736 | tf_op jit(solution)/shard_map/ppermute | solution.py:271
  798.2 44.0 %collective-permute-start.100 = (bf16[256,2048]{1,0:T(8,128)(2,1)S(1)}, bf16[256,2048]{1,0:T(8,128)(2,1)S(1)}, u32[]{:S(2)}, u32[]{:S(2)}) collective-permute-start(bf16[256,2048]{1,0:T(8,128)(2,1)S(1)} %add_convert_fusion.9), channel_id=1, source_target_pairs={{0,8},{1,9},{2,10},{3,11},{4,0},{5,1},{6,2},{7,3},{8,16},{9,17},{1... | collective-permute-start | bytes 3145736 | tf_op jit(solution)/shard_map/ppermute | solution.py:271
  800.0 42.1 %collective-permute-start.101 = (bf16[256,2048]{1,0:T(8,128)(2,1)S(1)}, bf16[256,2048]{1,0:T(8,128)(2,1)S(1)}, u32[]{:S(2)}, u32[]{:S(2)}) collective-permute-start(bf16[256,2048]{1,0:T(8,128)(2,1)S(1)} %add_convert_fusion.8), channel_id=1, source_target_pairs={{8,0},{9,1},{10,2},{11,3},{0,4},{1,5},{2,6},{3,7},{16,8},{17,9},{1... | collective-permute-start | bytes 3145736 | tf_op jit(solution)/shard_map/ppermute | solution.py:271
  835.0 55.9 %collective-permute-start.113 = (bf16[256,2048]{1,0:T(8,128)(2,1)}, bf16[256,2048]{1,0:T(8,128)(2,1)}, u32[]{:S(2)}, u32[]{:S(2)}) collective-permute-start(bf16[256,2048]{1,0:T(8,128)(2,1)} %pad_maximum_fusion.10), channel_id=1, source_target_pairs={{0,8},{1,9},{2,10},{3,11},{4,0},{5,1},{6,2},{7,3},{8,16},{9,17},{1... | collective-permute-start | bytes 3145736 | tf_op jit(solution)/shard_map/ppermute | solution.py:271
  837.6 53.4 %collective-permute-start.114 = (bf16[256,2048]{1,0:T(8,128)(2,1)}, bf16[256,2048]{1,0:T(8,128)(2,1)}, u32[]{:S(2)}, u32[]{:S(2)}) collective-permute-start(bf16[256,2048]{1,0:T(8,128)(2,1)} %pad_maximum_fusion.11), channel_id=1, source_target_pairs={{8,0},{9,1},{10,2},{11,3},{0,4},{1,5},{2,6},{3,7},{16,8},{17,9},{1... | collective-permute-start | bytes 3145736 | tf_op jit(solution)/shard_map/ppermute | solution.py:271
  849.0 54.8 %collective-permute-start.107 = (bf16[256,2048]{1,0:T(8,128)(2,1)}, bf16[256,2048]{1,0:T(8,128)(2,1)}, u32[]{:S(2)}, u32[]{:S(2)}) collective-permute-start(bf16[256,2048]{1,0:T(8,128)(2,1)} %slice.809), channel_id=1, source_target_pairs={{0,2},{1,3},{2,0},{3,1},{4,6},{5,7},{6,4},{7,5},{8,10},{9,11},{10,... | collective-permute-start | bytes 3145736 | tf_op jit(solution)/shard_map/ppermute | solution.py:271
  889.5 50.2 %collective-permute-start.104 = (bf16[256,2048]{1,0:T(8,128)(2,1)S(1)}, bf16[256,2048]{1,0:T(8,128)(2,1)S(1)}, u32[]{:S(2)}, u32[]{:S(2)}) collective-permute-start(bf16[256,2048]{1,0:T(8,128)(2,1)S(1)} %add_convert_fusion.6), channel_id=1, source_target_pairs={{0,8},{1,9},{2,10},{3,11},{4,0},{5,1},{6,2},{7,3},{8,16},{9,17},{1... | collective-permute-start | bytes 3145736 | tf_op jit(solution)/shard_map/ppermute | solution.py:271
  890.9 48.9 %collective-permute-start.105 = (bf16[256,2048]{1,0:T(8,128)(2,1)S(1)}, bf16[256,2048]{1,0:T(8,128)(2,1)S(1)}, u32[]{:S(2)}, u32[]{:S(2)}) collective-permute-start(bf16[256,2048]{1,0:T(8,128)(2,1)S(1)} %add_convert_fusion.5), channel_id=1, source_target_pairs={{8,0},{9,1},{10,2},{11,3},{0,4},{1,5},{2,6},{3,7},{16,8},{17,9},{1... | collective-permute-start | bytes 3145736 | tf_op jit(solution)/shard_map/ppermute | solution.py:271
  894.5 41.9 %collective-permute-start.121 = (bf16[256,2048]{1,0:T(8,128)(2,1)S(1)}, bf16[256,2048]{1,0:T(8,128)(2,1)S(1)}, u32[]{:S(2)}, u32[]{:S(2)}) collective-permute-start(bf16[256,2048]{1,0:T(8,128)(2,1)S(1)} %add_convert_fusion.3), channel_id=1, source_target_pairs={{0,8},{1,9},{2,10},{3,11},{4,0},{5,1},{6,2},{7,3},{8,16},{9,17},{1... | collective-permute-start | bytes 3145736 | tf_op jit(solution)/shard_map/ppermute | solution.py:271
  903.5 33.9 %collective-permute-start.122 = (bf16[256,2048]{1,0:T(8,128)(2,1)S(1)}, bf16[256,2048]{1,0:T(8,128)(2,1)S(1)}, u32[]{:S(2)}, u32[]{:S(2)}) collective-permute-start(bf16[256,2048]{1,0:T(8,128)(2,1)S(1)} %add_convert_fusion.2), channel_id=1, source_target_pairs={{8,0},{9,1},{10,2},{11,3},{0,4},{1,5},{2,6},{3,7},{16,8},{17,9},{1... | collective-permute-start | bytes 3145736 | tf_op jit(solution)/shard_map/ppermute | solution.py:271
  903.9 35.9 %collective-permute-start.106 = (bf16[256,2048]{1,0:T(8,128)(2,1)S(1)}, bf16[256,2048]{1,0:T(8,128)(2,1)S(1)}, u32[]{:S(2)}, u32[]{:S(2)}) collective-permute-start(bf16[256,2048]{1,0:T(8,128)(2,1)S(1)} %add_convert_fusion.7), channel_id=1, source_target_pairs={{0,1},{1,0},{2,3},{3,2},{4,5},{5,4},{6,7},{7,6},{8,9},{9,8},{10,11... | collective-permute-start | bytes 3145736 | tf_op jit(solution)/shard_map/ppermute | solution.py:271
  941.1 41.4 %collective-permute-start.130 = (bf16[64,2048]{1,0:T(8,128)(2,1)S(1)}, bf16[64,2048]{1,0:T(8,128)(2,1)S(1)}, u32[]{:S(2)}, u32[]{:S(2)}) collective-permute-start(bf16[64,2048]{1,0:T(8,128)(2,1)S(1)} %pad_maximum_fusion.25), channel_id=1, source_target_pairs={{0,0},{4,1},{2,2},{6,3},{1,4},{5,5},{3,6},{7,7},{8,8},{12,9},{10,1... | collective-permute-start | bytes 786440 | tf_op jit(solution)/shard_map/ppermute | solution.py:271
  949.2 34.1 %collective-permute-start.129 = (bf16[2,64,1536]{2,1,0:T(8,128)(2,1)S(1)}, bf16[2,64,1536]{2,1,0:T(8,128)(2,1)S(1)}, u32[]{:S(2)}, u32[]{:S(2)}) collective-permute-start(bf16[2,64,1536]{2,1,0:T(8,128)(2,1)S(1)} %pad_maximum_fusion.23), channel_id=1, source_target_pairs={{0,2},{1,3},{2,0},{3,1},{4,6},{5,7},{6,4},{7,5},{8,10},{9,11},{10,... | collective-permute-start | bytes 1179656 | tf_op jit(solution)/shard_map/ppermute | solution.py:271
  (295 other events, 4234.3 us)
